TPU v7x, 32 devices: a whole 2x2x4 slice. The times are simulated.
32 devices in a mesh: seq: 16 (over z, y, core), batch: 2 (over x).
Axes of the slice: x: 2, y: 2, z: 4, core: 2. Of those that a mesh axis runs over, the one named last changes fastest.
Arguments:
- tokens: bfloat16 [2, 2048, 1024], P('batch', 'seq'), may hold values from -6 to 6
- ln_gain: bfloat16 [1024], P(('seq', 'batch')), may hold values from 0.099609375 to 1.8984375
- ln_bias: bfloat16 [1024], P(('seq', 'batch')), may hold values from -3 to 3
- w_qkv: bfloat16 [1024, 3072], P(('seq', 'batch')), may hold values from -0.25 to 0.25
- b_qkv: bfloat16 [3072], P(('seq', 'batch')), may hold values from -2 to 2
- w_out: bfloat16 [1024, 1024], P(('seq', 'batch')), may hold values from -1 to 1
- w_up: bfloat16 [1024, 4096], P(('seq', 'batch')), may hold values from -0.1875 to 0.1875
- b_up: bfloat16 [4096], P(('seq', 'batch')), may hold values from -3 to 3
- w_down: bfloat16 [4096, 1024], P(('seq', 'batch')), may hold values from -0.125 to 0.125
- b_out: bfloat16 [1024], P(('seq', 'batch')), may hold values from -3 to 3
- cotangent: bfloat16 [2, 2048, 1024], P('batch', 'seq'), may hold values from -6 to 6
Outputs:
- out: bfloat16 [2, 2048, 1024], P('batch', 'seq')
- d_tokens: float32 [2, 2048, 1024], P('batch', 'seq')
- d_ln_gain: float32 [1024], P(('seq', 'batch'))
- d_ln_bias: float32 [1024], P(('seq', 'batch'))
- d_w_qkv: float32 [1024, 3072], P(('seq', 'batch'))
- d_b_qkv: float32 [3072], P(('seq', 'batch'))
- d_w_out: float32 [1024, 1024], P(('seq', 'batch'))
- d_w_up: float32 [1024, 4096], P(('seq', 'batch'))
- d_b_up: float32 [4096], P(('seq', 'batch'))
- d_w_down: float32 [4096, 1024], P(('seq', 'batch'))
- d_b_out: float32 [1024], P(('seq', 'batch'))
All inputs are finite; a program needn't handle non-finite values.
Results may differ from a plain program's by a relative error of at most 0.015.
Values may be sent and summed in bfloat16 or wider, within the bound.
A program may use at most 192 MiB of HBM per device.

v0:
```python
import math

import jax
import jax.numpy as jnp
from jax import lax
from jax.sharding import PartitionSpec as P

HEADS = 16
ROTARY = 16


eps_norm = 1e-05
neg_big = -1e30
rotary_base = 10000.0


def rotary_tables(positions, half_width):
    frequency = rotary_base ** (
        -(2.0 * jnp.arange(half_width, dtype=jnp.float32)) / (2.0 * half_width)
    )
    angles = positions[:, None] * frequency[None, :]
    return (jnp.cos(angles)[:, None, :], jnp.sin(angles)[:, None, :])


def rotate(section, cosine_table, sine_table):
    half_width = cosine_table.shape[-1]
    first_half = section[..., :half_width]
    second_half = section[..., half_width : 2 * half_width]
    return jnp.concatenate(
        [
            first_half * cosine_table - second_half * sine_table,
            second_half * cosine_table + first_half * sine_table,
            section[..., 2 * half_width :],
        ],
        -1,
    )


def exact_gelu(values):
    return jax.nn.gelu(values, approximate=False)


def contract_rows(left, right):
    return lax.dot_general(
        left, right, (((0,), (0,)), ((), ())), preferred_element_type=jnp.float32
    )


def times_transposed(left, right):
    return lax.dot_general(
        left, right, (((1,), (1,)), ((), ())), preferred_element_type=jnp.float32
    )


def masked_scores(queries, key_rows, query_pos, key_pos, score_scale):
    scores = (
        jnp.einsum("qhd,khd->hqk", queries, key_rows, preferred_element_type=jnp.float32)
        * score_scale
    )
    allowed = key_pos[None, :] <= query_pos[:, None]
    return jnp.where(allowed[None], scores, neg_big)


def split_blocks(flat_rows, block_rows, head_count, head_dim):
    length = flat_rows.shape[0]
    return flat_rows.reshape(length // block_rows, block_rows, head_count, head_dim)


def attend(queries, key_all, value_all, query_pos, score_scale, block_rows):
    head_count, head_dim = (queries.shape[1], queries.shape[2])
    length = key_all.shape[0]
    key_blocks = split_blocks(key_all, block_rows, head_count, head_dim)
    value_blocks = split_blocks(value_all, block_rows, head_count, head_dim)
    position_blocks = jnp.arange(length, dtype=jnp.int32).reshape(length // block_rows, block_rows)

    def statistics(state_in, entry):
        running_max, running_sum = state_in
        key_rows, key_pos = entry
        scores = masked_scores(queries, key_rows, query_pos, key_pos, score_scale)
        new_max = jnp.maximum(running_max, jnp.max(scores, -1))
        running_sum = running_sum * jnp.exp(running_max - new_max) + jnp.sum(
            jnp.exp(scores - new_max[..., None]), -1
        )
        return ((new_max, running_sum), None)

    start_state = (
        jnp.full((head_count, queries.shape[0]), neg_big, jnp.float32),
        jnp.zeros((head_count, queries.shape[0]), jnp.float32),
    )
    (running_max, running_sum), _ = lax.scan(statistics, start_state, (key_blocks, position_blocks))
    log_total = running_max + jnp.log(running_sum)

    def attend_accumulate(mixed_heads, entry):
        key_rows, value_rows, key_pos = entry
        scores = masked_scores(queries, key_rows, query_pos, key_pos, score_scale)
        probs_low = jnp.exp(scores - log_total[..., None]).astype(jnp.bfloat16)
        return (
            mixed_heads
            + jnp.einsum("hqk,khd->qhd", probs_low, value_rows, preferred_element_type=jnp.float32),
            None,
        )

    mixed_heads, _ = lax.scan(
        attend_accumulate,
        jnp.zeros(queries.shape, jnp.float32),
        (key_blocks, value_blocks, position_blocks),
    )
    return (mixed_heads, log_total)


def query_grads(
    queries,
    grad_heads,
    key_all,
    value_all,
    log_total,
    delta_rows,
    query_pos,
    score_scale,
    block_rows,
):
    head_count, head_dim = (queries.shape[1], queries.shape[2])
    length = key_all.shape[0]
    key_blocks = split_blocks(key_all, block_rows, head_count, head_dim)
    value_blocks = split_blocks(value_all, block_rows, head_count, head_dim)
    position_blocks = jnp.arange(length, dtype=jnp.int32).reshape(length // block_rows, block_rows)

    def query_accumulate(grad_queries, entry):
        key_rows, value_rows, key_pos = entry
        scores = masked_scores(queries, key_rows, query_pos, key_pos, score_scale)
        probs = jnp.exp(scores - log_total[..., None])
        grad_probs = jnp.einsum(
            "qhd,khd->hqk", grad_heads, value_rows, preferred_element_type=jnp.float32
        )
        grad_scores = (probs * (grad_probs - delta_rows[..., None])).astype(jnp.bfloat16)
        return (
            grad_queries
            + jnp.einsum("hqk,khd->qhd", grad_scores, key_rows, preferred_element_type=jnp.float32),
            None,
        )

    grad_queries, _ = lax.scan(
        query_accumulate,
        jnp.zeros(queries.shape, jnp.float32),
        (key_blocks, value_blocks, position_blocks),
    )
    return grad_queries * score_scale


def key_terms(
    queries,
    grad_heads,
    log_total,
    delta_rows,
    query_pos,
    key_rows,
    value_rows,
    key_pos,
    score_scale,
):
    scores = masked_scores(queries, key_rows, query_pos, key_pos, score_scale)
    probs = jnp.exp(scores - log_total[..., None])
    grad_probs = jnp.einsum(
        "qhd,khd->hqk", grad_heads, value_rows, preferred_element_type=jnp.float32
    )
    grad_scores = (probs * (grad_probs - delta_rows[..., None])).astype(jnp.bfloat16)
    grad_keys = (
        jnp.einsum("hqk,qhd->khd", grad_scores, queries, preferred_element_type=jnp.float32)
        * score_scale
    )
    grad_values = jnp.einsum(
        "hqk,qhd->khd", probs.astype(jnp.bfloat16), grad_heads, preferred_element_type=jnp.float32
    )
    key_count = key_rows.shape[0]
    return jnp.concatenate(
        [grad_keys.reshape(key_count, -1), grad_values.reshape(key_count, -1)], -1
    )


def local(tokens, ln_gain, ln_bias, w_qkv, b_qkv, w_out, w_up, b_up, w_down, b_out, cotangent):
    seq_count, tok_rows, model_width = tokens.shape
    head_count = HEADS
    head_dim = model_width // head_count
    score_scale = head_dim ** (-0.5)
    length = tok_rows * lax.axis_size("seq")
    block_rows = math.gcd(length, 512)
    token_count = seq_count * tok_rows
    owned_shards = (ln_gain, ln_bias, w_qkv, b_qkv, w_out, w_up, b_up, w_down, b_out)
    norm_gain, norm_shift, wqkv, bqkv, wout, wup, bup, wdown, bout = (
        lax.all_gather(owned_shards[0], ("seq", "batch"), axis=0, tiled=True),
        lax.all_gather(owned_shards[1], ("seq", "batch"), axis=0, tiled=True),
        lax.all_gather(owned_shards[2], ("seq", "batch"), axis=0, tiled=True),
        lax.all_gather(owned_shards[3], ("seq", "batch"), axis=0, tiled=True),
        lax.all_gather(owned_shards[4], ("seq", "batch"), axis=0, tiled=True),
        lax.all_gather(owned_shards[5], ("seq", "batch"), axis=0, tiled=True),
        lax.all_gather(owned_shards[6], ("seq", "batch"), axis=0, tiled=True),
        lax.all_gather(owned_shards[7], ("seq", "batch"), axis=0, tiled=True),
        lax.all_gather(owned_shards[8], ("seq", "batch"), axis=0, tiled=True),
    )
    inputs = tokens.reshape(token_count, model_width).astype(jnp.float32)
    average = jnp.mean(inputs, -1, keepdims=True)
    centered = inputs - average
    inv_root = lax.rsqrt(jnp.mean(centered * centered, -1, keepdims=True) + eps_norm)
    unit_rows = centered * inv_root
    normed = (unit_rows * norm_gain.astype(jnp.float32) + norm_shift.astype(jnp.float32)).astype(
        jnp.bfloat16
    )
    joined_qkv = (
        jnp.dot(normed, wqkv, preferred_element_type=jnp.float32) + bqkv.astype(jnp.float32)
    ).reshape(seq_count, tok_rows, 3, head_count, head_dim)
    query_pos = lax.axis_index("seq") * tok_rows + jnp.arange(tok_rows, dtype=jnp.int32)
    cosine_table, sine_table = rotary_tables(query_pos.astype(jnp.float32), ROTARY // 2)
    queries = rotate(joined_qkv[:, :, 0], cosine_table, sine_table).astype(jnp.bfloat16)
    key_local = rotate(joined_qkv[:, :, 1], cosine_table, sine_table).astype(jnp.bfloat16)
    value_local = joined_qkv[:, :, 2].astype(jnp.bfloat16)
    key_all, value_all = (
        lax.all_gather(
            key_local.reshape(seq_count, tok_rows, model_width), "seq", axis=1, tiled=True
        ),
        lax.all_gather(
            value_local.reshape(seq_count, tok_rows, model_width), "seq", axis=1, tiled=True
        ),
    )

    def forward_sequence(entry):
        query_seq, key_seq, value_seq = entry
        return attend(query_seq, key_seq, value_seq, query_pos, score_scale, block_rows)

    mixed_heads, log_total = lax.map(forward_sequence, (queries, key_all, value_all))
    mixed_low = mixed_heads.reshape(token_count, model_width).astype(jnp.bfloat16)
    attn_out = jnp.dot(mixed_low, wout, preferred_element_type=jnp.float32)
    up_proj = jnp.dot(normed, wup, preferred_element_type=jnp.float32) + bup.astype(jnp.float32)
    activation = exact_gelu(up_proj).astype(jnp.bfloat16)
    mlp_out = jnp.dot(activation, wdown, preferred_element_type=jnp.float32)
    result = (inputs + attn_out + mlp_out + bout.astype(jnp.float32)).astype(jnp.bfloat16)
    norm_gain, norm_shift, wqkv, bqkv, wout, wup, bup, wdown, bout = (
        lax.all_gather(owned_shards[0], ("seq", "batch"), axis=0, tiled=True),
        lax.all_gather(owned_shards[1], ("seq", "batch"), axis=0, tiled=True),
        lax.all_gather(owned_shards[2], ("seq", "batch"), axis=0, tiled=True),
        lax.all_gather(owned_shards[3], ("seq", "batch"), axis=0, tiled=True),
        lax.all_gather(owned_shards[4], ("seq", "batch"), axis=0, tiled=True),
        lax.all_gather(owned_shards[5], ("seq", "batch"), axis=0, tiled=True),
        lax.all_gather(owned_shards[6], ("seq", "batch"), axis=0, tiled=True),
        lax.all_gather(owned_shards[7], ("seq", "batch"), axis=0, tiled=True),
        lax.all_gather(owned_shards[8], ("seq", "batch"), axis=0, tiled=True),
    )
    cotangent_rows = cotangent.reshape(token_count, model_width)
    cotangent_f = cotangent_rows.astype(jnp.float32)
    grad_bout = jnp.sum(cotangent_f, 0)
    grad_wout = contract_rows(mixed_low, cotangent_rows)
    grad_wdown = contract_rows(activation, cotangent_rows)
    grad_act = times_transposed(cotangent_rows, wdown)
    _, gelu_back = jax.vjp(exact_gelu, up_proj)
    grad_up = gelu_back(grad_act)[0].astype(jnp.bfloat16)
    grad_wup = contract_rows(normed, grad_up)
    grad_bup = jnp.sum(grad_up.astype(jnp.float32), 0)
    grad_heads = (
        times_transposed(cotangent_rows, wout)
        .astype(jnp.bfloat16)
        .reshape(seq_count, tok_rows, head_count, head_dim)
    )
    delta_rows = jnp.swapaxes(jnp.sum(grad_heads.astype(jnp.float32) * mixed_heads, -1), 1, 2)

    def backward_sequence(entry):
        query_seq, grad_seq, key_seq, value_seq, total_seq, delta_seq = entry
        return query_grads(
            query_seq,
            grad_seq,
            key_seq,
            value_seq,
            total_seq,
            delta_seq,
            query_pos,
            score_scale,
            block_rows,
        )

    grad_queries = lax.map(
        backward_sequence, (queries, grad_heads, key_all, value_all, log_total, delta_rows)
    )
    row_count = tok_rows * lax.axis_size("seq")
    sub_rows = math.gcd(row_count, 512)

    def one_block(block_index):
        first_key = block_index * sub_rows
        key_pos = first_key + jnp.arange(sub_rows, dtype=jnp.int32)

        def one_sequence(entry):
            query_seq, grad_seq, total_seq, delta_seq, key_seq, value_seq = entry
            key_rows = lax.dynamic_slice_in_dim(key_seq, first_key, sub_rows, 0).reshape(
                sub_rows, head_count, head_dim
            )
            value_rows = lax.dynamic_slice_in_dim(value_seq, first_key, sub_rows, 0).reshape(
                sub_rows, head_count, head_dim
            )
            return key_terms(
                query_seq,
                grad_seq,
                total_seq,
                delta_seq,
                query_pos,
                key_rows,
                value_rows,
                key_pos,
                score_scale,
            )

        per_sequence = lax.map(
            one_sequence, (queries, grad_heads, log_total, delta_rows, key_all, value_all)
        )
        return jnp.swapaxes(per_sequence, 0, 1)

    block_terms = lax.map(one_block, jnp.arange(row_count // sub_rows, dtype=jnp.int32))
    summed = lax.psum_scatter(
        block_terms.reshape(row_count, seq_count, 2 * model_width).astype(jnp.bfloat16),
        "seq",
        scatter_dimension=0,
        tiled=True,
    ).astype(jnp.float32)
    key_grads_all = jnp.swapaxes(summed, 0, 1)
    grad_keys = key_grads_all[..., :model_width].reshape(seq_count, tok_rows, head_count, head_dim)
    grad_values = key_grads_all[..., model_width:].reshape(
        seq_count, tok_rows, head_count, head_dim
    )
    grad_q_turned = rotate(grad_queries, cosine_table, -sine_table)
    grad_k_turned = rotate(grad_keys, cosine_table, -sine_table)
    grad_joined = (
        jnp.stack([grad_q_turned, grad_k_turned, grad_values], 2)
        .reshape(token_count, 3 * model_width)
        .astype(jnp.bfloat16)
    )
    grad_wqkv = contract_rows(normed, grad_joined)
    grad_bqkv = jnp.sum(grad_joined.astype(jnp.float32), 0)
    grad_normed = times_transposed(grad_joined, wqkv) + times_transposed(grad_up, wup)
    grad_gain = jnp.sum(grad_normed * unit_rows, 0)
    grad_shift = jnp.sum(grad_normed, 0)
    grad_unit = grad_normed * norm_gain.astype(jnp.float32)
    grad_inputs = cotangent_f + inv_root * (
        grad_unit
        - jnp.mean(grad_unit, -1, keepdims=True)
        - unit_rows * jnp.mean(grad_unit * unit_rows, -1, keepdims=True)
    )
    owner_grads = (
        lax.psum_scatter(grad_gain, ("seq", "batch"), scatter_dimension=0, tiled=True),
        lax.psum_scatter(grad_shift, ("seq", "batch"), scatter_dimension=0, tiled=True),
        lax.psum_scatter(grad_wqkv, ("seq", "batch"), scatter_dimension=0, tiled=True),
        lax.psum_scatter(grad_bqkv, ("seq", "batch"), scatter_dimension=0, tiled=True),
        lax.psum_scatter(grad_wout, ("seq", "batch"), scatter_dimension=0, tiled=True),
        lax.psum_scatter(grad_wup, ("seq", "batch"), scatter_dimension=0, tiled=True),
        lax.psum_scatter(grad_bup, ("seq", "batch"), scatter_dimension=0, tiled=True),
        lax.psum_scatter(grad_wdown, ("seq", "batch"), scatter_dimension=0, tiled=True),
        lax.psum_scatter(grad_bout, ("seq", "batch"), scatter_dimension=0, tiled=True),
    )
    return (
        result.reshape(seq_count, tok_rows, model_width),
        grad_inputs.reshape(seq_count, tok_rows, model_width),
        owner_grads[0],
        owner_grads[1],
        owner_grads[2],
        owner_grads[3],
        owner_grads[4],
        owner_grads[5],
        owner_grads[6],
        owner_grads[7],
        owner_grads[8],
    )


def solution(mesh):
    in_specs = (
        P("batch", "seq", None),
        P(("seq", "batch")),
        P(("seq", "batch")),
        P(("seq", "batch"), None),
        P(("seq", "batch")),
        P(("seq", "batch"), None),
        P(("seq", "batch"), None),
        P(("seq", "batch")),
        P(("seq", "batch"), None),
        P(("seq", "batch")),
        P("batch", "seq", None),
    )
    out_specs = (
        P("batch", "seq", None),
        P("batch", "seq", None),
        P(("seq", "batch")),
        P(("seq", "batch")),
        P(("seq", "batch"), None),
        P(("seq", "batch")),
        P(("seq", "batch"), None),
        P(("seq", "batch"), None),
        P(("seq", "batch")),
        P(("seq", "batch"), None),
        P(("seq", "batch")),
    )
    return jax.shard_map(local, mesh=mesh, in_specs=in_specs, out_specs=out_specs, check_vma=False)
```

profile of v0, /device:TPU:0, one launch (start us, length us, event | category | flops | bytes accessed | tf_op | source)
XLA Modules:
  0.0 1648.2 jit_solution(10833509972765885334)
XLA Ops:
  12.1 42.5 %all-reduce.10 = (bf16[1024]{0:T(1024)(128)(2,1)S(1)}, bf16[1024]{0:T(1024)(128)(2,1)S(1)}, bf16[3072]{0:T(1024)(128)(2,1)S(1)}, bf16[1024]{0:T(1024)(128)(2,1)}) all-reduce(bf16[1024]{0:T(1024)(128)(2,1)S(1)} %dynamic-update-slice.1, bf16[1024]{0:T(1024)(128)(2,1)S(1)} %dynamic-update-slice, ...), channel_id=1, replica_groups=mesh['seq'=16,'batch'=2] {'seq','batch'}, use_global_device_ids=true, to_apply=%add.1 | all-reduce | flops 6144 | bytes 24576
  57.0 26.4 %all-gather.8.cloned.1.call-done = bf16[1024,3072]{1,0:T(8,128)(2,1)} async-done(((bf16[32,3072]{1,0:T(8,128)(2,1)}), bf16[1024,3072]{1,0:T(8,128)(2,1)}) %all-gather.8.cloned.1.call-update) | async-done | bytes 6291472 | tf_op jit(solution)/shard_map/all_gather | solution.py:192
  90.2 51.1 %all-gather.14.cloned.1.call-done = bf16[1024,1024]{1,0:T(8,128)(2,1)} async-done(((bf16[32,1024]{1,0:T(8,128)(2,1)}), bf16[1024,1024]{1,0:T(8,128)(2,1)}) %all-gather.14.cloned.1.call-update) | async-done | bytes 2097168 | tf_op jit(solution)/shard_map/all_gather | solution.py:194
  144.1 52.1 %all-gather.12.cloned.1.call-done = bf16[1,2048,1024]{1,2,0:T(8,128)(2,1)} async-done(((bf16[1,128,1024]{1,2,0:T(8,128)(2,1)}), bf16[1,2048,1024]{1,2,0:T(8,128)(2,1)}) %all-gather.12.cloned.1.call-update) | async-done | bytes 4194320 | tf_op jit(solution)/shard_map/all_gather | solution.py:217
  196.2 7.9 reshape.558
  204.1 5.3 copy.55
  209.4 29.6 %while.70 = (s32[]{:T(128)}, f32[16,128]{1,0:T(8,128)S(1)}, f32[16,128]{1,0:T(8,128)S(1)}, s32[4,512]{1,0:T(4,128)S(1)}, bf16[4,512,16,64]{1,3,2,0:T(8,128)(2,1)...) while((s32[]{:T(128)}, f32[16,128]{1,0:T(8,128)S(1)}, ...), condition=%wide.region_5.6_spmd.clone, body=%wide.region_2.5_spmd.clone.sunk | while | flops 141633664 | bytes 10010224 | solution.py:90
  238.9 11.3 all-gather.10.cloned.1.call-done
  250.2 7.9 reshape.554
  258.1 5.1 copy.54
  263.2 13.9 while.71
  278.0 77.7 %while.69 = (s32[]{:T(128)}, bf16[4,512,1,2048]{3,1,0,2:T(8,128)(2,1)}, s32[4]{0:T(128)S(1)}, bf16[1,2048,1024]{1,2,0:T(8,128)(2,1)}, bf16[1,128,16,64]{1,3,2,0:...) while((s32[]{:T(128)}, ...), condition=%wide.region_12.13_spmd.clone, body=%wide.region_11.12_spmd.clone.sunk | while | flops 552665728 | bytes 39024440 | solution.py:313
  360.0 37.2 %while.72 = (s32[]{:T(128)}, f32[128,16,64]{0,2,1:T(8,128)S(1)}, bf16[4,512,16,64]{1,3,2,0:T(8,128)(2,1)}, s32[4,512]{1,0:T(4,128)S(1)}, bf16[128,16,64]{0,2,1:T...) while((s32[]{:T(128)}, f32[128,16,64]{0,2,1:T(8,128)S(1)}, ...), condition=%wide.region_10.11_spmd.clone, body=%wide.region_9.10_spmd.clone.sunk | while | flops 409272448 | bytes 13263495 | solution.py:142
  364.1 5.4 fusion.189
  373.7 5.2 fusion.189
  383.1 5.0 fusion.189
  392.3 4.8 fusion.189
  397.2 61.5 %reduce-scatter.6.cloned.1.call-done = bf16[128,1,2048]{2,0,1:T(8,128)(2,1)} async-done(((bf16[2048,1,2048]{2,0,1:T(8,128)(2,1)}), bf16[128,1,2048]{2,0,1:T(8,128)(2,1)}) %reduce-scatter.6.cloned.1.call-update) | async-done | bytes 524304 | tf_op jit(solution)/shard_map/reduce_scatter | solution.py:314
  461.1 6.4 fusion.100
  468.2 67.1 %all-gather = bf16[32,1,128]{2,1,0:T(2,128)(2,1)S(1)} all-gather(bf16[1,1,128]{2,1,0:T(2,128)(2,1)S(1)} %bitcast.349), channel_id=1, replica_groups=mesh['seq'=16,'batch'=2] {'seq','batch'}, dimensions={0}, use_global_device_ids=true | all-gather | bytes 8448 | tf_op jit(solution)/shard_map/all_gather | solution.py:196
  538.7 9.1 multiply_convert_fusion
  547.9 69.9 %all-gather.18.cloned.1.call-done = bf16[4096,1024]{1,0:T(8,128)(2,1)} async-done(((bf16[128,1024]{1,0:T(8,128)(2,1)}), bf16[4096,1024]{1,0:T(8,128)(2,1)}) %all-gather.18.cloned.1.call-update) | async-done | bytes 8388624 | tf_op jit(solution)/shard_map/all_gather | solution.py:197
  617.8 9.8 convert_reduce_fusion
  628.6 8.2 fusion.116
  637.1 8.1 fusion.102
  652.0 5.1 fusion.121
  657.1 6.5 fusion.92
  664.7 40.2 %all-reduce.9 = (f32[1024]{0:T(1024)S(1)}, f32[1024]{0:T(1024)S(1)}, f32[3072]{0:T(1024)S(1)}, f32[4096]{0:T(1024)S(1)}, f32[1024]{0:T(1024)S(1)}) all-reduce(f32[1024]{0:T(1024)S(1)} %get-tuple-element.475, f32[1024]{0:T(1024)S(1)} %get-tuple-element.478, ...), channel_id=3, replica_groups=mesh['seq'=16,'batch'=2] {'seq','batch'}, use_global_device_ids=true, to_apply=%region_17.18.clone | all-reduce | flops 10240 | bytes 81920
  707.9 53.5 %reduce-scatter.10.cloned.1.call-done = f32[32,1024]{1,0:T(8,128)} async-done(((f32[1024,1024]{1,0:T(8,128)}), f32[32,1024]{1,0:T(8,128)}) %reduce-scatter.10.cloned.1.call-update) | async-done | bytes 131088 | tf_op jit(solution)/shard_map/reduce_scatter | solution.py:348
  761.4 159.1 %reduce-scatter.8.cloned.1.call-done = f32[32,3072]{1,0:T(8,128)} async-done(((f32[1024,3072]{1,0:T(8,128)}), f32[32,3072]{1,0:T(8,128)}) %reduce-scatter.8.cloned.1.call-update) | async-done | bytes 393232 | tf_op jit(solution)/shard_map/reduce_scatter | solution.py:346
  920.5 359.3 %reduce-scatter.12.cloned.1.call-done = f32[32,4096]{1,0:T(8,128)} async-done(((f32[1024,4096]{1,0:T(8,128)}), f32[32,4096]{1,0:T(8,128)}) %reduce-scatter.12.cloned.1.call-update) | async-done | bytes 524304 | tf_op jit(solution)/shard_map/reduce_scatter | solution.py:349
  1279.8 361.6 %reduce-scatter.14.cloned.1.call-done = f32[128,1024]{1,0:T(8,128)} async-done(((f32[4096,1024]{1,0:T(8,128)}), f32[128,1024]{1,0:T(8,128)}) %reduce-scatter.14.cloned.1.call-update) | async-done | bytes 524304 | tf_op jit(solution)/shard_map/reduce_scatter | solution.py:351
  (246 shorter events, 174.8 us)
Async XLA Ops:
  7.2 76.2 %all-gather.8.cloned.1.call-start = ((), (), s32[]{:S(2)}) async-start(), calls=%async_computation.5 | async-start | bytes 6488064 | tf_op jit(solution)/shard_map/all_gather | solution.py:192
  7.9 133.5 %all-gather.14.cloned.1.call-start = ((), (), s32[]{:S(2)}) async-start(), calls=%async_computation.8 | async-start | bytes 2162688 | tf_op jit(solution)/shard_map/all_gather | solution.py:194
  8.7 187.6 %all-gather.12.cloned.1.call-start = ((), (), s32[]{:S(2)}) async-start(), calls=%async_computation.7 | async-start | bytes 4456448 | tf_op jit(solution)/shard_map/all_gather | solution.py:217
  87.8 53.6 %copy-start.4 = (bf16[1,128,1024]{2,1,0:T(8,128)(2,1)S(1)}, bf16[1,128,1024]{2,1,0:T(8,128)(2,1)}, u32[]{:S(2)}) copy-start(bf16[1,128,1024]{2,1,0:T(8,128)(2,1)} %param.29) | copy-start | bytes 786436
  88.8 161.4 %all-gather.10.cloned.1.call-start = ((), (), s32[]{:S(2)}) async-start(), calls=%async_computation.6 | async-start | bytes 4456448 | tf_op jit(solution)/shard_map/all_gather | solution.py:220
  89.6 369.1 %reduce-scatter.6.cloned.1.call-start = ((), (), s32[]{:S(2)}) async-start(), calls=%async_computation.11 | async-start | bytes 8912896 | tf_op jit(solution)/shard_map/reduce_scatter | solution.py:314
  278.0 5.9 copy-start.1
  278.0 10.2 copy-start.9
  294.1 3.2 copy-start.2
  294.1 3.2 copy-start.10
  297.4 5.9 copy-start.1
  297.4 10.2 copy-start.9
  313.6 3.2 copy-start.2
  313.6 3.2 copy-start.10
  316.8 5.9 copy-start.1
  316.8 10.2 copy-start.9
  333.0 3.2 copy-start.2
  333.0 3.2 copy-start.10
  336.2 5.9 copy-start.1
  336.2 10.2 copy-start.9
  352.4 3.3 copy-start.2
  352.4 3.3 copy-start.10
  355.7 1.4 copy-start.5
  355.7 1.4 copy-start.8
  355.7 183.0 %all-gather.16.cloned.1.call-start = ((), (), s32[]{:S(2)}) async-start(), calls=%async_computation.9 | async-start | bytes 8650752 | tf_op jit(solution)/shard_map/all_gather | solution.py:195
  356.3 261.5 %all-gather.18.cloned.1.call-start = ((), (), s32[]{:S(2)}) async-start(), calls=%async_computation.10 | async-start | bytes 8650752 | tf_op jit(solution)/shard_map/all_gather | solution.py:197
  357.0 404.3 %reduce-scatter.10.cloned.1.call-start = ((), (), s32[]{:S(2)}) async-start(), calls=%async_computation.13 | async-start | bytes 4325376 | tf_op jit(solution)/shard_map/reduce_scatter | solution.py:348
  359.9 560.6 %reduce-scatter.8.cloned.1.call-start = ((), (), s32[]{:S(2)}) async-start(), calls=%async_computation.12 | async-start | bytes 12976128 | tf_op jit(solution)/shard_map/reduce_scatter | solution.py:346
  467.5 812.2 %reduce-scatter.12.cloned.1.call-start = ((), (), s32[]{:S(2)}) async-start(), calls=%async_computation.14 | async-start | bytes 17301504 | tf_op jit(solution)/shard_map/reduce_scatter | solution.py:349
  636.8 1004.6 %reduce-scatter.14.cloned.1.call-start = ((), (), s32[]{:S(2)}) async-start(), calls=%async_computation.15 | async-start | bytes 17301504 | tf_op jit(solution)/shard_map/reduce_scatter | solution.py:351
  645.9 4.8 copy-start.3
  652.0 5.1 copy-start.7
  (4 other events, 3.3 us)
Sparse Core Ops, SparseCore 0:
  10.9 72.4 all-gather.7
  86.4 54.9 all-gather.13
  144.1 52.0 all-gather.11
  198.8 51.3 all-gather.9
  355.8 102.8 reduce-scatter.5
  461.6 77.1 all-gather.15
  541.7 76.0 all-gather.17
  620.6 140.6 reduce-scatter.9
  768.0 152.4 reduce-scatter.7
  923.3 356.4 reduce-scatter.11
  1282.7 358.6 reduce-scatter.13
where the time goes:
time: 1650 us
  waiting for transfers between devices  1210 us (73%)
  matrix products  176 us (11%)
  blocking collectives  150 us (9%)
  local copies, waits for them, and re-layouts  69.3 us (4%)
  other arithmetic  21.9 us (1%)
    reduce_scatter x1, waiting for transfers between devices, local(): lax.psum_scatter(grad_wdown, ('seq', 'batch'), scatter_dimension=0, tiled...  362 us
    reduce_scatter x1, waiting for transfers between devices, local(): lax.psum_scatter(grad_wup, ('seq', 'batch'), scatter_dimension=0, tiled=T...  359 us
    reduce_scatter x1, waiting for transfers between devices, local(): lax.psum_scatter(grad_wqkv, ('seq', 'batch'), scatter_dimension=0, tiled=...  159 us
    unnamed x2, blocking collectives  82.7 us
    all_gather x1, waiting for transfers between devices, local(): lax.all_gather(owned_shards[7], ('seq', 'batch'), axis=0, tiled=True)  69.9 us
    all_gather x1, blocking collectives, local(): lax.all_gather(owned_shards[6], ('seq', 'batch'), axis=0, tiled=True)  67.1 us
    reduce_scatter x1, waiting for transfers between devices, local(): lax.psum_scatter(block_terms.reshape(row_count, seq_count, 2 * model_widt...  61.5 us
    reduce_scatter x1, waiting for transfers between devices, local(): lax.psum_scatter(grad_wout, ('seq', 'batch'), scatter_dimension=0, tiled=...  53.5 us
  transfers between devices with their start and end apart: 11, of which 11 were waited for; matrix products, arithmetic and copies ran while one was open for 10% of the time, Pallas kernels for 0%

commit v1 on v0

--- a/solution.py
+++ b/solution.py
@@ -2,7 +2,10 @@
 
 import jax
 import jax.numpy as jnp
+import numpy as np
 from jax import lax
+from jax.experimental import pallas as pl
+from jax.experimental.pallas import tpu as pltpu
 from jax.sharding import PartitionSpec as P
 
 HEADS = 16
@@ -366,6 +369,717 @@
     )
 
 
+MESH = pl.DeviceIdType.MESH
+F32, BF16 = jnp.float32, jnp.bfloat16
+TOK = 128
+BT = 256
+MODEL = 1024
+SEQ = 16
+CHIPS = 8
+UP = 256
+HD = 64
+WIDE = 512
+VEC = 448
+GRADS = 448
+
+
+def dot(left, right):
+    return jnp.dot(left, right, preferred_element_type=F32)
+
+
+def dot_nt(left, right):
+    return lax.dot_general(left, right, (((1,), (1,)), ((), ())), preferred_element_type=F32)
+
+
+def lanes(block):
+    if isinstance(block, int):
+        return slice(block * BT, (block + 1) * BT)
+    return pl.ds(pl.multiple_of(block * BT, BT), BT)
+
+
+def turn(rows, cosine, sine):
+    first, second = rows[0:8], rows[8:16]
+    return jnp.concatenate(
+        [first * cosine - second * sine, second * cosine + first * sine, rows[16:]], 0
+    )
+
+
+def remote(src, dst, send_sem, recv_sem, device):
+    return pltpu.make_async_remote_copy(
+        src_ref=src,
+        dst_ref=dst,
+        send_sem=send_sem,
+        recv_sem=recv_sem,
+        device_id=device,
+        device_id_type=MESH,
+    )
+
+
+def fused(
+    tokens, cot, w_qkv, w_out, w_up, w_down, vec, cost, sint,
+    out, d_tok, d_qkv, d_out, d_up, d_down, d_vec,
+    tok, g, wsend, wc, wct, wd, gv, bct, normed, unit, amt, dactt, qt, kt, vt, k, v, sbuf, e,
+    linv, ot, gt, dost, delta, dkt, dvt, part, rc1, ry1, rzl1, rzr1, rc2, ry2, rzl2, rzr2, tmp,
+    dgain, dshift, dbout, dwct, dwd, dsend, drecv, dws, xrecv, arecv,
+    w_ss, w_rs, x_ss, x_rs, wd_ss, wd_rs, t_ss, t_rs, g_ss, g_rs,
+    c1_ss, c1_rs, y1_ss, y1_rs, zp1_ss, zl1_rs, zm1_ss, zr1_rs,
+    c2_ss, c2_rs, y2_ss, y2_rs, zp2_ss, zl2_rs, zm2_ss, zr2_rs,
+    d_ss, d_rs, dx_ss, dx_rs, a_ss, a_rs,
+):
+    s = lax.axis_index("seq")
+    b = lax.axis_index("batch")
+    z, y, c = s // 4, (s // 2) % 2, s % 2
+    oy, oc, ob = 1 - y, 1 - c, 1 - b
+    sib = (s + 1 - 2 * c, b)
+    yn = (s + 2 - 4 * y, b)
+    zp = (lax.rem(s + 4, SEQ), b)
+    zm = (lax.rem(s + SEQ - 4, SEQ), b)
+    xn = (s, ob)
+    offsets = [(dz, dy, dc) for dz in (0, 1, 3, 2) for dy in (0, 1) for dc in (0, 1)][1:]
+
+    def shifted(offset, sign):
+        dz, dy, dc = offset
+        return (
+            4 * lax.rem(z + 4 + sign * dz, 4)
+            + 2 * lax.rem(y + 2 + sign * dy, 2)
+            + lax.rem(c + 2 + sign * dc, 2)
+        )
+
+    high = z // 2
+    zo = [z, z + 1 - 2 * lax.rem(z, 2), 2 - high, 3 - 3 * high]
+
+    barrier = pltpu.get_barrier_semaphore()
+    for off in offsets:
+        pl.semaphore_signal(
+            barrier, inc=1, device_id=(shifted(off, 1), b), device_id_type=MESH
+        )
+    pl.semaphore_signal(barrier, inc=1, device_id=xn, device_id_type=MESH)
+
+    for t in range(SEQ):
+        wsend[t] = jnp.concatenate(
+            [
+                w_up[:, UP * t : UP * (t + 1)],
+                w_qkv[:, HD * t : HD * (t + 1)],
+                w_qkv[:, MODEL + HD * t : MODEL + HD * (t + 1)],
+                w_qkv[:, 2 * MODEL + HD * t : 2 * MODEL + HD * (t + 1)],
+                vec[...],
+            ],
+            1,
+        )
+    wc[2 * s + b] = wsend[s]
+    tok[s] = tokens[...]
+    g[s] = cot[...]
+    down_own = pl.ds(pl.multiple_of(128 * b, 128), 128)
+    down_other = pl.ds(pl.multiple_of(128 * ob, 128), 128)
+    out_own = pl.ds(pl.multiple_of(UP + 32 * b, 32), 32)
+    out_other = pl.ds(pl.multiple_of(UP + 32 * ob, 32), 32)
+    wd[down_own] = w_down[...]
+    wd[out_own] = w_out[...]
+    pl.semaphore_wait(barrier, SEQ)
+
+    def w_copy(source, target):
+        return remote(
+            wsend.at[target], wc.at[2 * source + b], w_ss.at[target], w_rs.at[source], (target, b)
+        )
+
+    def x_copy(source, plane):
+        return remote(
+            wc.at[2 * source + plane], wc.at[2 * source + plane],
+            x_ss.at[source], x_rs.at[source], xn,
+        )
+
+    wd_copies = [
+        remote(w_down, wd.at[down_own], wd_ss.at[0], wd_rs.at[0], xn),
+        remote(w_out, wd.at[out_own], wd_ss.at[1], wd_rs.at[1], xn),
+    ]
+
+    def gather(buf, ss, rs):
+        def send(shard, way, device):
+            return remote(buf.at[shard], buf.at[shard], ss.at[way, shard], rs.at[shard], device)
+
+        def arrived(shard):
+            send(shard, 0, sib).wait_recv()
+
+        def own(act):
+            @pl.when(z < 3)
+            def _():
+                act(send(s, 0, zp))
+
+            @pl.when(z > 0)
+            def _():
+                act(send(s, 1, zm))
+
+            act(send(s, 2, yn))
+            act(send(s, 3, sib))
+
+        def on_z(t, act):
+            shard = 4 * zo[t] + 2 * y + c
+
+            @pl.when(jnp.logical_and(zo[t] < z, z < 3))
+            def _():
+                act(send(shard, 0, zp))
+
+            @pl.when(jnp.logical_and(zo[t] > z, z > 0))
+            def _():
+                act(send(shard, 1, zm))
+
+            act(send(shard, 2, yn))
+            act(send(shard, 3, sib))
+
+        def on_y(t, act):
+            act(send(4 * zo[t] + 2 * oy + c, 3, sib))
+
+        start = lambda copy: copy.start()
+        finish = lambda copy: copy.wait_send()
+
+        def step_z(t):
+            arrived(4 * zo[t] + 2 * y + c)
+            on_z(t, start)
+
+        def step_y(t):
+            arrived(4 * zo[t] + 2 * oy + c)
+            on_y(t, start)
+
+        def step_core(t, row):
+            arrived(4 * zo[t] + 2 * row + oc)
+
+        def drain():
+            own(finish)
+            for t in range(1, 4):
+                on_z(t, finish)
+            for t in range(4):
+                on_y(t, finish)
+
+        return (lambda: own(start)), step_z, step_y, step_core, drain
+
+    tok_own, tok_z, tok_y, tok_core, tok_drain = gather(tok, t_ss, t_rs)
+    g_own, g_z, g_y, g_core, g_drain = gather(g, g_ss, g_rs)
+
+    for off in offsets:
+        w_copy(s, shifted(off, 1)).start()
+    x_copy(s, b).start()
+    tok_own()
+    for off in offsets:
+        source = shifted(off, -1)
+        w_copy(source, s).wait_recv()
+        x_copy(source, b).start()
+    for copy in wd_copies:
+        copy.start()
+    tok_z(1)
+    tok_y(0)
+    for t in range(SEQ):
+        x_copy(t, ob).wait_recv()
+
+    wct[...] = wc[...].reshape(MODEL, WIDE).T
+    rows = wct[VEC : VEC + 16, :].astype(F32)
+    gv[0:1] = rows[0:1]
+    gv[1:2] = rows[1:2]
+    gv[2:3] = rows[2:3]
+    cols = []
+    for half in range(2):
+        tail = wc[2 * s + half][:, VEC - HD :].astype(F32)
+        for i in range(4):
+            cols.append(tail[:, HD + 3 + i : HD + 4 + i])
+    lane_of = lax.broadcasted_iota(jnp.int32, (32, 128), 1)
+    for which in range(3):
+        for half in range(2):
+            chunk = 32 * which + 2 * s + half
+            tail = wc[chunk // 3][:, VEC - HD :].astype(F32)
+            cols.append(
+                jnp.sum(jnp.where(lane_of == HD + 7 + lax.rem(chunk, 3), tail, 0.0), 1, keepdims=True)
+            )
+    bct[...] = jnp.concatenate(cols, 0)
+
+    def project(i):
+        x = tok[pl.ds(2 * i, 2)].reshape(BT, MODEL).astype(F32)
+        centered = x - jnp.mean(x, -1, keepdims=True)
+        inv = lax.rsqrt(jnp.mean(centered * centered, -1, keepdims=True) + eps_norm)
+        u = centered * inv
+        n = (u * gv[0:1] + gv[1:2]).astype(BF16)
+        normed[i] = n
+        unit[i] = u.astype(BF16)
+        jt = dot_nt(wct[0:VEC], n) + bct[...]
+        up = jt[0:UP]
+        half = 0.5 + 0.5 * lax.erf(up * 0.7071067811865476)
+        at = lanes(i)
+        amt[0:UP, at] = (up * half).astype(BF16)
+        dactt[:, at] = half + up * (jnp.exp(-0.5 * up * up) * 0.3989422804014327)
+        cs, sn = cost[:, at], sint[:, at]
+        qt[:, at] = (turn(jt[256:320], cs, sn) * 0.125).astype(BF16)
+        keys = turn(jt[320:384], cs, sn)
+        kt[:, at] = keys.astype(BF16)
+        vt[:, at] = jt[384:448].astype(BF16)
+        k[i] = keys.T.astype(BF16)
+        v[i] = jt[384:448].T.astype(BF16)
+
+    def chip_of(t, row):
+        return 2 * zo[t] + row
+
+    for t in range(4):
+        tok_core(t, y)
+        project(chip_of(t, y))
+        if t + 2 < 4:
+            tok_z(t + 2)
+        if t == 1:
+            g_own()
+        tok_core(t, oy)
+        project(chip_of(t, oy))
+        if t + 1 < 4:
+            tok_y(t + 1)
+
+    def attend_fwd(qb):
+        at = lanes(qb)
+        base = qb * (qb + 1) // 2
+        q = qt[:, at]
+        top = None
+        for kb in range(qb + 1):
+            st = dot(k[kb], q)
+            if kb == qb:
+                key_at = lax.broadcasted_iota(jnp.int32, (BT, BT), 0)
+                query_at = lax.broadcasted_iota(jnp.int32, (BT, BT), 1)
+                st = jnp.where(key_at <= query_at, st, neg_big)
+            sbuf[kb] = st
+            here = jnp.max(st, 0, keepdims=True)
+            top = here if top is None else jnp.maximum(top, here)
+        total = jnp.zeros((1, BT), F32)
+        o = jnp.zeros((HD, BT), F32)
+        for kb in range(qb + 1):
+            ee = jnp.exp(sbuf[kb] - top)
+            total = total + jnp.sum(ee, 0, keepdims=True)
+            eb = ee.astype(BF16)
+            e[base + kb] = eb
+            o = o + dot(vt[:, lanes(kb)], eb)
+        li = 1.0 / total
+        linv[:, at] = li
+        o = o * li
+        ot[:, at] = o
+        amt[UP : UP + HD, at] = o.astype(BF16)
+
+    def reducer(rc, ry, rzl, rzr, c_ss, c_rs, y_ss, y_rs, zp_ss, zl_rs, zm_ss, zr_rs):
+        order = [zo[3], zo[2], zo[1], zo[0]]
+
+        def core_copy(t, row, color):
+            chip = 2 * order[t] + row
+            return remote(
+                part.at[2 * chip + color], rc.at[chip], c_ss.at[chip], c_rs.at[chip], sib
+            )
+
+        def y_copy(t, row):
+            return remote(
+                rc.at[2 * order[t] + row], ry.at[order[t]], y_ss.at[order[t]], y_rs.at[order[t]], yn
+            )
+
+        def zp_copy(t):
+            at = order[t]
+            return remote(rc.at[2 * at + y], rzl.at[at], zp_ss.at[at], zl_rs.at[at], zp)
+
+        def zm_copy(t):
+            at = order[t]
+            return remote(rc.at[2 * at + y], rzr.at[at], zm_ss.at[at], zr_rs.at[at], zm)
+
+        def send_core(t, row):
+            core_copy(t, row, oc).start()
+
+        def send_y(t):
+            chip = 2 * order[t] + oy
+            core_copy(t, oy, oc).wait_recv()
+            rc[chip] = (rc[chip].astype(F32) + part[2 * chip + c].astype(F32)).astype(BF16)
+            y_copy(t, oy).start()
+
+        def sum_here(t):
+            chip = 2 * order[t] + y
+            core_copy(t, y, oc).wait_recv()
+            y_copy(t, y).wait_recv()
+            tmp[...] = (
+                rc[chip].astype(F32) + part[2 * chip + c].astype(F32) + ry[order[t]].astype(F32)
+            )
+
+        def add_left(t):
+            zp_copy(t).wait_recv()
+            tmp[...] += rzl[order[t]].astype(F32)
+
+        def add_right(t):
+            zm_copy(t).wait_recv()
+            tmp[...] += rzr[order[t]].astype(F32)
+
+        def pass_on(t):
+            at = order[t]
+            sum_here(t)
+
+            @pl.when(jnp.logical_and(at > z, z > 0))
+            def _():
+                add_left(t)
+
+            @pl.when(jnp.logical_and(at < z, z < 3))
+            def _():
+                add_right(t)
+
+            rc[2 * at + y] = tmp[...].astype(BF16)
+
+            @pl.when(at > z)
+            def _():
+                zp_copy(t).start()
+
+            @pl.when(at < z)
+            def _():
+                zm_copy(t).start()
+
+        def last():
+            sum_here(3)
+
+            @pl.when(z > 0)
+            def _():
+                add_left(3)
+
+            @pl.when(z < 3)
+            def _():
+                add_right(3)
+
+        def drain_core():
+            for t in range(4):
+                for row in (oy, y):
+                    core_copy(t, row, oc).wait_send()
+
+        def drain():
+            for t in range(4):
+                y_copy(t, oy).wait_send()
+            for t in range(3):
+                at = order[t]
+
+                @pl.when(at > z)
+                def _():
+                    zp_copy(t).wait_send()
+
+                @pl.when(at < z)
+                def _():
+                    zm_copy(t).wait_send()
+
+        return order, send_core, send_y, pass_on, last, drain_core, drain
+
+    order, core1, y1, pass1, last1, drain_core1, drain1 = reducer(
+        rc1, ry1, rzl1, rzr1, c1_ss, c1_rs, y1_ss, y1_rs, zp1_ss, zl1_rs, zm1_ss, zr1_rs
+    )
+    _, core2, y2, pass2, last2, drain_core2, drain2 = reducer(
+        rc2, ry2, rzl2, rzr2, c2_ss, c2_rs, y2_ss, y2_rs, zp2_ss, zl2_rs, zm2_ss, zr2_rs
+    )
+
+    def out_block(t, row):
+        i = 2 * order[t] + row
+        part[pl.ds(2 * i, 2)] = (
+            dot(amt[:, lanes(i)].T, wd[...]).astype(BF16).reshape(2, TOK, MODEL)
+        )
+        core1(t, row)
+
+    def grads_at(i):
+        gb = g[pl.ds(2 * i, 2)].reshape(BT, MODEL)
+        at = lanes(i)
+        r = dot_nt(wd[...], gb)
+        gt[0:UP, at] = (r[0:UP] * dactt[:, at]).astype(BF16)
+        li = linv[:, at]
+        gm = r[UP : UP + HD]
+        dost[:, at] = (gm * li).astype(BF16)
+        delta[:, at] = jnp.sum(gm * ot[:, at], 0, keepdims=True) * li
+        dbout[...] += jnp.sum(gb.astype(F32).reshape(BT // 8, 8, MODEL), 0)
+
+    def attend_bwd(qb):
+        at = lanes(qb)
+        base = qb * (qb + 1) // 2
+        do, q, de = dost[:, at], qt[:, at], delta[:, at]
+        dq = jnp.zeros((HD, BT), F32)
+        for kb in range(qb + 1):
+            ks = lanes(kb)
+            eb = e[base + kb]
+            dp = dot(v[kb], do)
+            ds = (eb.astype(F32) * (dp - de)).astype(BF16)
+            dv = dot_nt(do, eb)
+            dk = dot_nt(q, ds)
+            if kb == qb:
+                dvt[:, ks] = dv
+                dkt[:, ks] = dk
+            else:
+                dvt[:, ks] += dv
+                dkt[:, ks] += dk
+            dq = dq + dot(kt[:, ks], ds)
+        gt[256:320, at] = turn(dq * 0.125, cost[:, at], -sint[:, at]).astype(BF16)
+
+    def norm_grads(t, row):
+        i = 2 * order[t] + row
+        gn = dot(gt[:, lanes(i)].T, wct[0:GRADS])
+        part[pl.ds(2 * i, 2)] = gn.astype(BF16).reshape(2, TOK, MODEL)
+        core2(t, row)
+        dshift[...] += jnp.sum(gn.reshape(BT // 8, 8, MODEL), 0)
+        dgain[...] += jnp.sum((gn * unit[i].astype(F32)).reshape(BT // 8, 8, MODEL), 0)
+
+    dgain[...] = jnp.zeros_like(dgain)
+    dshift[...] = jnp.zeros_like(dshift)
+    dbout[...] = jnp.zeros_like(dbout)
+    for copy in wd_copies:
+        copy.wait_send()
+    remote(w_down, wd.at[down_other], wd_ss.at[0], wd_rs.at[0], xn).wait_recv()
+    remote(w_out, wd.at[out_other], wd_ss.at[1], wd_rs.at[1], xn).wait_recv()
+
+    g_z(1)
+    g_y(0)
+    for qb in range(CHIPS):
+        attend_fwd(qb)
+    g_z(2)
+    g_core(0, y)
+    grads_at(chip_of(0, y))
+    out_block(0, oy)
+    out_block(0, y)
+    out_block(1, oy)
+    out_block(1, y)
+    g_y(1)
+    g_core(0, oy)
+    grads_at(chip_of(0, oy))
+    g_core(1, y)
+    grads_at(chip_of(1, y))
+    out_block(2, oy)
+    out_block(2, y)
+    out_block(3, oy)
+    out_block(3, y)
+    g_z(3)
+    for t in range(4):
+        y1(t)
+    g_core(1, oy)
+    grads_at(chip_of(1, oy))
+    g_core(2, y)
+    grads_at(chip_of(2, y))
+    g_y(2)
+    g_core(2, oy)
+    grads_at(chip_of(2, oy))
+    g_core(3, y)
+    grads_at(chip_of(3, y))
+    g_y(3)
+    g_core(3, oy)
+    grads_at(chip_of(3, oy))
+
+    for qb in range(CHIPS):
+        attend_bwd(qb)
+    pass1(0)
+    gt[320:384, :] = turn(dkt[...], cost[...], -sint[...]).astype(BF16)
+    gt[384:448, :] = dvt[...].astype(BF16)
+
+    gg = g.reshape(SEQ * TOK, MODEL)
+    for n in range(4):
+        dwd[:, lanes(n)] = dot(amt[...], gg[:, lanes(n)])
+    dsend[0:128] = dwd[down_other].astype(BF16)
+    dsend[128:160] = dwd[out_other].astype(BF16)
+    d_copy = remote(dsend, drecv, d_ss, d_rs, xn)
+    d_copy.start()
+
+    pass1(1)
+    pass1(2)
+    last1()
+    out[...] = (tmp[...] + tokens[...].astype(F32) + gv[2:3]).astype(BF16)
+    drain_core1()
+    for t in range(4):
+        norm_grads(t, oy)
+        norm_grads(t, y)
+    for t in range(4):
+        y2(t)
+
+    nn = normed.reshape(SEQ * TOK, MODEL)
+    for n in range(4):
+        dwct[0:GRADS, lanes(n)] = dot(gt[...], nn[:, lanes(n)])
+    dwct[GRADS:WIDE] = jnp.zeros((WIDE - GRADS, MODEL), F32)
+    dwct[VEC : VEC + 1] = jnp.sum(dgain[...], 0, keepdims=True)
+    dwct[VEC + 1 : VEC + 2] = jnp.sum(dshift[...], 0, keepdims=True)
+    dwct[VEC + 2 : VEC + 3] = jnp.sum(dbout[...], 0, keepdims=True)
+    bias_col = jnp.sum(gt[...].astype(F32), 1, keepdims=True)
+    bias_cols = jnp.concatenate(
+        [jnp.zeros((32, HD + 3), F32)]
+        + [bias_col[32 * n : 32 * (n + 1)] for n in range(14)]
+        + [jnp.zeros((32, 128 - HD - 17), F32)],
+        1,
+    )
+    for j in range(2 * SEQ // 4):
+        turned = dwct[:, 128 * j : 128 * (j + 1)].T
+        for i in range(4):
+            piece = turned[32 * i : 32 * (i + 1)]
+            dev = 4 * j + i
+            dws[dev % 2, dev // 2, :, 0:384] = piece[:, 0:384].astype(BF16)
+            dws[dev % 2, dev // 2, :, 384:512] = (piece[:, 384:512] + bias_cols).astype(BF16)
+    dx_copy = remote(dws.at[ob], xrecv, dx_ss, dx_rs, xn)
+    dx_copy.start()
+    pass2(0)
+    pass2(1)
+    dx_copy.wait_recv()
+    dws[b] = (dws[b].astype(F32) + xrecv[...].astype(F32)).astype(BF16)
+
+    def a_copy(source, target):
+        return remote(
+            dws.at[b, target], arecv.at[source], a_ss.at[target], a_rs.at[source], (target, b)
+        )
+
+    for off in offsets:
+        a_copy(s, shifted(off, 1)).start()
+    arecv[s] = dws[b, s]
+    d_copy.wait_recv()
+    d_down[...] = dwd[down_own] + drecv[0:128].astype(F32)
+    d_out[...] = dwd[out_own] + drecv[128:160].astype(F32)
+    pass2(2)
+    last2()
+
+    x = tokens[...].astype(F32)
+    centered = x - jnp.mean(x, -1, keepdims=True)
+    inv = lax.rsqrt(jnp.mean(centered * centered, -1, keepdims=True) + eps_norm)
+    u = centered * inv
+    gu = tmp[...] * gv[0:1]
+    d_tok[...] = cot[...].astype(F32) + inv * (
+        gu - jnp.mean(gu, -1, keepdims=True) - u * jnp.mean(gu * u, -1, keepdims=True)
+    )
+
+    for off in offsets:
+        a_copy(shifted(off, -1), s).wait_recv()
+    sums = jnp.zeros((32, 128), F32)
+    for t in range(0, SEQ, 2):
+        even, odd = arecv[t].astype(F32), arecv[t + 1].astype(F32)
+        d_up[:, UP * t : UP * (t + 1)] = even[:, 0:UP]
+        d_up[:, UP * (t + 1) : UP * (t + 2)] = odd[:, 0:UP]
+        for which in range(3):
+            lo = UP + HD * which
+            d_qkv[:, MODEL * which + HD * t : MODEL * which + HD * (t + 2)] = jnp.concatenate(
+                [even[:, lo : lo + HD], odd[:, lo : lo + HD]], 1
+            )
+        sums = sums + even[:, 384:512] + odd[:, 384:512]
+    mine = arecv[s][:, 384:512].astype(F32)
+    picked = [sums[:, HD : HD + 1], sums[:, HD + 1 : HD + 2], mine[:, HD + 2 : HD + 3]]
+
+    def pick(block, lane):
+        return jnp.sum(jnp.where(lane_of == lane, block, 0.0), 1, keepdims=True)
+
+    for i in range(4):
+        picked.append(pick(mine, HD + 3 + 4 * b + i))
+    for i in range(3):
+        chunk = 3 * (2 * s + b) + i
+        block = arecv[lax.rem(chunk, 32) // 2][:, 384:512].astype(F32)
+        picked.append(pick(block, HD + 3 + 8 + 2 * (chunk // 32) + lax.rem(chunk, 2)))
+    d_vec[...] = jnp.concatenate(picked + [jnp.zeros((32, 118), F32)], 1)
+
+    for off in offsets:
+        w_copy(s, shifted(off, 1)).wait_send()
+        a_copy(s, shifted(off, 1)).wait_send()
+    for t in range(SEQ):
+        x_copy(t, b).wait_send()
+    tok_drain()
+    g_drain()
+    drain1()
+    drain_core2()
+    drain2()
+    d_copy.wait_send()
+    dx_copy.wait_send()
+
+
+def fast_local(
+    tokens, ln_gain, ln_bias, w_qkv, b_qkv, w_out, w_up, b_up, w_down, b_out, cotangent
+):
+    vec = jnp.concatenate([ln_gain, ln_bias, b_out, b_up, b_qkv]).reshape(10, 32).T
+    vec = jnp.pad(vec, ((0, 0), (0, HD - 10)))
+    length = SEQ * TOK
+    frequency = rotary_base ** (-(2.0 * np.arange(8)) / 16.0)
+    angles = frequency.astype(np.float32)[:, None] * np.arange(length, dtype=np.float32)[None]
+    cost = jnp.asarray(np.cos(angles.astype(np.float64)).astype(np.float32))
+    sint = jnp.asarray(np.sin(angles.astype(np.float64)).astype(np.float32))
+    vm = pl.BlockSpec(memory_space=pltpu.VMEM)
+    shape = jax.ShapeDtypeStruct
+    dma = pltpu.SemaphoreType.DMA
+
+    def reduce_buffers():
+        return [
+            pltpu.VMEM((CHIPS, TOK, MODEL), BF16),
+            pltpu.VMEM((4, TOK, MODEL), BF16),
+            pltpu.VMEM((4, TOK, MODEL), BF16),
+            pltpu.VMEM((4, TOK, MODEL), BF16),
+        ]
+
+    reduce_sems = [dma((8,)), dma((8,))] + [dma((4,))] * 6
+    results = pl.pallas_call(
+        fused,
+        out_shape=[
+            shape((TOK, MODEL), BF16),
+            shape((TOK, MODEL), F32),
+            shape((32, 3 * MODEL), F32),
+            shape((32, MODEL), F32),
+            shape((32, 4 * MODEL), F32),
+            shape((128, MODEL), F32),
+            shape((32, 128), F32),
+        ],
+        in_specs=[vm] * 9,
+        out_specs=[vm] * 7,
+        scratch_shapes=[
+            pltpu.VMEM((SEQ, TOK, MODEL), BF16),
+            pltpu.VMEM((SEQ, TOK, MODEL), BF16),
+            pltpu.VMEM((SEQ, 32, WIDE), BF16),
+            pltpu.VMEM((2 * SEQ, 32, WIDE), BF16),
+            pltpu.VMEM((WIDE, MODEL), BF16),
+            pltpu.VMEM((UP + HD, MODEL), BF16),
+            pltpu.VMEM((8, MODEL), F32),
+            pltpu.VMEM((VEC, 1), F32),
+            pltpu.VMEM((CHIPS, BT, MODEL), BF16),
+            pltpu.VMEM((CHIPS, BT, MODEL), BF16),
+            pltpu.VMEM((UP + HD, length), BF16),
+            pltpu.VMEM((UP, length), F32),
+            pltpu.VMEM((HD, length), BF16),
+            pltpu.VMEM((HD, length), BF16),
+            pltpu.VMEM((HD, length), BF16),
+            pltpu.VMEM((CHIPS, BT, HD), BF16),
+            pltpu.VMEM((CHIPS, BT, HD), BF16),
+            pltpu.VMEM((CHIPS, BT, BT), F32),
+            pltpu.VMEM((36, BT, BT), BF16),
+            pltpu.VMEM((1, length), F32),
+            pltpu.VMEM((HD, length), F32),
+            pltpu.VMEM((GRADS, length), BF16),
+            pltpu.VMEM((HD, length), BF16),
+            pltpu.VMEM((1, length), F32),
+            pltpu.VMEM((HD, length), F32),
+            pltpu.VMEM((HD, length), F32),
+            pltpu.VMEM((SEQ, TOK, MODEL), BF16),
+        ]
+        + reduce_buffers()
+        + reduce_buffers()
+        + [
+            pltpu.VMEM((TOK, MODEL), F32),
+            pltpu.VMEM((8, MODEL), F32),
+            pltpu.VMEM((8, MODEL), F32),
+            pltpu.VMEM((8, MODEL), F32),
+            pltpu.VMEM((WIDE, MODEL), F32),
+            pltpu.VMEM((UP + HD, MODEL), F32),
+            pltpu.VMEM((160, MODEL), BF16),
+            pltpu.VMEM((160, MODEL), BF16),
+            pltpu.VMEM((2, SEQ, 32, WIDE), BF16),
+            pltpu.VMEM((SEQ, 32, WIDE), BF16),
+            pltpu.VMEM((SEQ, 32, WIDE), BF16),
+            dma((SEQ,)), dma((SEQ,)), dma((SEQ,)), dma((SEQ,)), dma((2,)), dma((2,)),
+            dma((4, SEQ)), dma((SEQ,)), dma((4, SEQ)), dma((SEQ,)),
+        ]
+        + reduce_sems
+        + reduce_sems
+        + [dma, dma, dma, dma, dma((SEQ,)), dma((SEQ,))],
+        compiler_params=pltpu.CompilerParams(
+            collective_id=0, has_side_effects=True, vmem_limit_bytes=62 * 2**20
+        ),
+    )(
+        tokens.reshape(TOK, MODEL), cotangent.reshape(TOK, MODEL),
+        w_qkv, w_out, w_up, w_down, vec, cost, sint,
+    )
+    out, d_tok, d_qkv, d_out, d_up, d_down, d_vec = results
+    vectors = d_vec[:, 0:10].T
+    return (
+        out.reshape(tokens.shape),
+        d_tok.reshape(tokens.shape),
+        vectors[0],
+        vectors[1],
+        d_qkv,
+        vectors[7:10].reshape(96),
+        d_out,
+        d_up,
+        vectors[3:7].reshape(128),
+        d_down,
+        vectors[2],
+    )
+
+
 def solution(mesh):
     in_specs = (
         P("batch", "seq", None),
@@ -393,4 +1107,6 @@
         P(("seq", "batch"), None),
         P(("seq", "batch")),
     )
-    return jax.shard_map(local, mesh=mesh, in_specs=in_specs, out_specs=out_specs, check_vma=False)
+    fits = mesh.shape["seq"] == SEQ and mesh.shape["batch"] == 2
+    body = fast_local if fits else local
+    return jax.shard_map(body, mesh=mesh, in_specs=in_specs, out_specs=out_specs, check_vma=False)

time: 1650 us -> 164 us (0.10)
  waiting for transfers between devices: 1210 us -> 0 us
  matrix products: 176 us -> 0 us
  blocking collectives: 150 us -> 0 us
  Pallas kernels: 0 us -> 149 us
  local copies, waits for them, and re-layouts: 69.3 us -> 13.8 us
  other arithmetic: 21.9 us -> 0 us
    reduce_scatter x5 -> x0, waiting for transfers between devices: 995 us -> none  [the longest x1 362 us: local(): lax.psum_scatter(grad_wdown, ('seq', 'batch'), scatter_dimension=0, tiled...]
    all_gather x6 -> x0, waiting for transfers between devices: 214 us -> none  [the longest x1 69.9 us: local(): lax.all_gather(owned_shards[7], ('seq', 'batch'), axis=0, tiled=True)]
    dot_general x40 -> x0, matrix products: 176 us -> none  [the longest x12 43.5 us: masked_scores(): jnp.einsum('qhd,khd->hqk', queries, key_rows, preferred_element_type=jnp....]
    pallas_call x0 -> x1, Pallas kernels: none -> 149 us  [fast_local(): pl.pallas_call(fused, out_shape=[shape((TOK, MODEL), BF16), shape((TOK, M...]
    unnamed x2 -> x0, blocking collectives: 82.7 us -> none
    all_gather x1 -> x0, blocking collectives: 67.1 us -> none  [local(): lax.all_gather(owned_shards[6], ('seq', 'batch'), axis=0, tiled=True)]
    dynamic_update_slice x8 -> x0, local copies, waits for them, and re-layouts: 22.7 us -> none  [local(): lax.map(one_block, jnp.arange(row_count // sub_rows, dtype=jnp.int32))]
    reduce_sum x9 -> x0, other arithmetic: 16.7 us -> none  [the longest x4 12.1 us: statistics(): jnp.sum(jnp.exp(scores - new_max[..., None]), -1)]
  transfers between devices with their start and end apart: 11 -> 0, of which waited for: 11 -> 0; matrix products, arithmetic and copies ran while one was open for 10% -> 0% of each run, Pallas kernels for 0% -> 0%
where the time goes in v1:
time: 164 us; the launch traced here: 163 us
  Pallas kernels  149 us (91%)
  local copies, waits for them, and re-layouts  13.8 us (8%)
    pallas_call x1, Pallas kernels, fast_local(): pl.pallas_call(fused, out_shape=[shape((TOK, MODEL), BF16), shape((TOK, M...  149 us
    unnamed x16, local copies, waits for them, and re-layouts  6.53 us
    concatenate x1, local copies, waits for them, and re-layouts, fast_local(): jnp.concatenate([ln_gain, ln_bias, b_out, b_up, b_qkv]).reshape(10, 32)  3.43 us

profile of v1, /device:TPU:0, one launch (start us, length us, event | category | flops | bytes accessed | tf_op | source)
XLA Modules:
  0.0 163.3 jit_solution(2850510892761082457)
XLA Ops:
  0.6 3.4 %concatenate.3 = bf16[320]{0:T(512)(128)(2,1)S(1)} concatenate(bf16[32]{0:T(256)(128)(2,1)} %param.14, bf16[32]{0:T(256)(128)(2,1)} %param.15, bf16[32]{0:T(256)(128)(2,1)} %param.22, bf16[128]{0:T(256)(128)(2,1)} %param.20, bf16[96]{0:T(256)(128)(2,1)} %param.17), dimensions={0} | concatenate | bytes 1280 | tf_op jit(solution)/shard_map/concatenate | solution.py:977
  4.1 0.1 reshape.45
  4.2 0.1 copy.26
  4.3 0.6 pad.4.vec
  4.9 148.8 %shard_map.212 = (bf16[128,1024]{1,0:T(8,128)(2,1)}, f32[128,1024]{1,0:T(8,128)}, f32[32,3072]{1,0:T(8,128)}, f32[32,1024]{1,0:T(8,128)}, f32[32,4096]{1,0:T(8,1...) custom-call(bf16[128,1024]{1,0:T(8,128)(2,1)} %bitcast.9, bf16[128,1024]{1,0:T(8,128)(2,1)} %bitcast.10, ...), custom_call_target="tpu_custom_call" | custom-call | tf_op jit(solution)/shard_map/pallas_call | solution.py:997
  153.7 0.0 copy-start.2
  153.7 0.8 slice_bitcast_fusion
  154.5 0.7 slice_reduce_fusion
  155.2 0.1 slice.26
  155.3 0.1 copy.27
  155.4 0.6 reshape.48
  156.0 0.1 slice.27
  156.0 0.1 copy.28
  156.1 0.6 reshape.49
  156.7 1.7 %copy.35 = bf16[1,128,1024]{2,1,0:T(8,128)(2,1)} copy(bf16[1,128,1024]{2,1,0:T(8,128)(2,1)} %bitcast.8) | data formatting | bytes 524288
  158.4 0.0 copy-done.2
  158.4 0.0 copy-start.3
  158.4 0.8 copy.36
  159.2 0.4 copy-done.3
  159.6 0.0 copy-start.4
  159.6 0.0 copy-start.1
  159.6 0.7 copy.37
  160.3 0.2 copy-done.4
  160.6 0.7 copy.38
  161.2 0.0 copy-done.1
  161.2 0.0 copy-start
  161.2 0.8 copy.39
  162.0 0.4 copy-done
  162.5 0.8 copy.40
Async XLA Ops:
  153.7 4.7 %copy-start.2 = (f32[128,1024]{1,0:T(8,128)S(1)}, f32[128,1024]{1,0:T(8,128)}, u32[]{:S(2)}) copy-start(f32[128,1024]{1,0:T(8,128)} %get-tuple-element.19) | copy-start | bytes 1572868
  158.4 1.2 copy-start.3
  159.6 1.0 copy-start.4
  159.6 1.7 %copy-start.1 = (f32[32,4096]{1,0:T(8,128)S(1)}, f32[32,4096]{1,0:T(8,128)}, u32[]{:S(2)}) copy-start(f32[32,4096]{1,0:T(8,128)} %get-tuple-element.46) | copy-start | bytes 1572868
  161.2 1.2 copy-start

commit v2 on v1

--- a/solution.py
+++ b/solution.py
@@ -416,15 +416,15 @@
 
 
 def fused(
-    tokens, cot, w_qkv, w_out, w_up, w_down, vec, cost, sint,
-    out, d_tok, d_qkv, d_out, d_up, d_down, d_vec,
+    tokens, cot, w_qkv, w_out, w_up, w_down, gain, shift, bout, bup, bqkv, cost, sint,
+    out, gn_sum, norm_gain, d_rows, arecv, ln_sums,
     tok, g, wsend, wc, wct, wd, gv, bct, normed, unit, amt, dactt, qt, kt, vt, k, v, sbuf, e,
-    linv, ot, gt, dost, delta, dkt, dvt, part, rc1, ry1, rzl1, rzr1, rc2, ry2, rzl2, rzr2, tmp,
-    dgain, dshift, dbout, dwct, dwd, dsend, drecv, dws, xrecv, arecv,
+    linv, ot, gt, dost, delta, dkt, dvt, part1, rc1, ry1, rzl1, rzr1, rc2, ry2, rzl2, rzr2, tmp,
+    dgain, dshift, dbout, dwct, dwd, dsend, drecv, dws, xrecv, vsend, vrecv, vparts,
     w_ss, w_rs, x_ss, x_rs, wd_ss, wd_rs, t_ss, t_rs, g_ss, g_rs,
     c1_ss, c1_rs, y1_ss, y1_rs, zp1_ss, zl1_rs, zm1_ss, zr1_rs,
     c2_ss, c2_rs, y2_ss, y2_rs, zp2_ss, zl2_rs, zm2_ss, zr2_rs,
-    d_ss, d_rs, dx_ss, dx_rs, a_ss, a_rs,
+    d_ss, d_rs, dx_ss, dx_rs, a_ss, a_rs, vx_ss, vx_rs, v_ss, v_rs,
 ):
     s = lax.axis_index("seq")
     b = lax.axis_index("batch")
@@ -455,6 +455,11 @@
         )
     pl.semaphore_signal(barrier, inc=1, device_id=xn, device_id_type=MESH)
 
+    vectors = [gain[...], shift[...], bout[...]]
+    vectors += [bup[:, 32 * i : 32 * (i + 1)] for i in range(4)]
+    vectors += [bqkv[:, 32 * i : 32 * (i + 1)] for i in range(3)]
+    vec = jnp.concatenate([w.astype(F32) for w in vectors] + [jnp.zeros((6, 32), F32)], 0).T
+    vec = jnp.concatenate([vec, jnp.zeros((32, HD - 16), F32)], 1).astype(BF16)
     for t in range(SEQ):
         wsend[t] = jnp.concatenate(
             [
@@ -462,7 +467,7 @@
                 w_qkv[:, HD * t : HD * (t + 1)],
                 w_qkv[:, MODEL + HD * t : MODEL + HD * (t + 1)],
                 w_qkv[:, 2 * MODEL + HD * t : 2 * MODEL + HD * (t + 1)],
-                vec[...],
+                vec,
             ],
             1,
         )
@@ -555,18 +560,18 @@
     tok_own, tok_z, tok_y, tok_core, tok_drain = gather(tok, t_ss, t_rs)
     g_own, g_z, g_y, g_core, g_drain = gather(g, g_ss, g_rs)
 
+    tok_own()
     for off in offsets:
         w_copy(s, shifted(off, 1)).start()
     x_copy(s, b).start()
-    tok_own()
+    tok_z(1)
+    tok_y(0)
     for off in offsets:
         source = shifted(off, -1)
         w_copy(source, s).wait_recv()
         x_copy(source, b).start()
     for copy in wd_copies:
         copy.start()
-    tok_z(1)
-    tok_y(0)
     for t in range(SEQ):
         x_copy(t, ob).wait_recv()
 
@@ -627,6 +632,14 @@
         if t + 1 < 4:
             tok_y(t + 1)
 
+    def e_put(n, block):
+        m, at = 2 * (n // 4), 256 * (n % 4)
+        e[m : m + 2, :, at : at + 256] = block.reshape(2, TOK, BT)
+
+    def e_get(n):
+        m, at = 2 * (n // 4), 256 * (n % 4)
+        return e[m : m + 2, :, at : at + 256].reshape(BT, BT)
+
     def attend_fwd(qb):
         at = lanes(qb)
         base = qb * (qb + 1) // 2
@@ -647,7 +660,7 @@
             ee = jnp.exp(sbuf[kb] - top)
             total = total + jnp.sum(ee, 0, keepdims=True)
             eb = ee.astype(BF16)
-            e[base + kb] = eb
+            e_put(base + kb, eb)
             o = o + dot(vt[:, lanes(kb)], eb)
         li = 1.0 / total
         linv[:, at] = li
@@ -655,7 +668,7 @@
         ot[:, at] = o
         amt[UP : UP + HD, at] = o.astype(BF16)
 
-    def reducer(rc, ry, rzl, rzr, c_ss, c_rs, y_ss, y_rs, zp_ss, zl_rs, zm_ss, zr_rs):
+    def reducer(part, rc, ry, rzl, rzr, c_ss, c_rs, y_ss, y_rs, zp_ss, zl_rs, zm_ss, zr_rs):
         order = [zo[3], zo[2], zo[1], zo[0]]
 
         def core_copy(t, row, color):
@@ -757,15 +770,15 @@
         return order, send_core, send_y, pass_on, last, drain_core, drain
 
     order, core1, y1, pass1, last1, drain_core1, drain1 = reducer(
-        rc1, ry1, rzl1, rzr1, c1_ss, c1_rs, y1_ss, y1_rs, zp1_ss, zl1_rs, zm1_ss, zr1_rs
+        part1, rc1, ry1, rzl1, rzr1, c1_ss, c1_rs, y1_ss, y1_rs, zp1_ss, zl1_rs, zm1_ss, zr1_rs
     )
     _, core2, y2, pass2, last2, drain_core2, drain2 = reducer(
-        rc2, ry2, rzl2, rzr2, c2_ss, c2_rs, y2_ss, y2_rs, zp2_ss, zl2_rs, zm2_ss, zr2_rs
+        e, rc2, ry2, rzl2, rzr2, c2_ss, c2_rs, y2_ss, y2_rs, zp2_ss, zl2_rs, zm2_ss, zr2_rs
     )
 
     def out_block(t, row):
         i = 2 * order[t] + row
-        part[pl.ds(2 * i, 2)] = (
+        part1[pl.ds(2 * i, 2)] = (
             dot(amt[:, lanes(i)].T, wd[...]).astype(BF16).reshape(2, TOK, MODEL)
         )
         core1(t, row)
@@ -788,7 +801,7 @@
         dq = jnp.zeros((HD, BT), F32)
         for kb in range(qb + 1):
             ks = lanes(kb)
-            eb = e[base + kb]
+            eb = e_get(base + kb)
             dp = dot(v[kb], do)
             ds = (eb.astype(F32) * (dp - de)).astype(BF16)
             dv = dot_nt(do, eb)
@@ -805,7 +818,7 @@
     def norm_grads(t, row):
         i = 2 * order[t] + row
         gn = dot(gt[:, lanes(i)].T, wct[0:GRADS])
-        part[pl.ds(2 * i, 2)] = gn.astype(BF16).reshape(2, TOK, MODEL)
+        e[pl.ds(2 * i, 2)] = gn.astype(BF16).reshape(2, TOK, MODEL)
         core2(t, row)
         dshift[...] += jnp.sum(gn.reshape(BT // 8, 8, MODEL), 0)
         dgain[...] += jnp.sum((gn * unit[i].astype(F32)).reshape(BT // 8, 8, MODEL), 0)
@@ -856,41 +869,20 @@
 
     for qb in range(CHIPS):
         attend_bwd(qb)
-    pass1(0)
     gt[320:384, :] = turn(dkt[...], cost[...], -sint[...]).astype(BF16)
     gt[384:448, :] = dvt[...].astype(BF16)
-
-    gg = g.reshape(SEQ * TOK, MODEL)
-    for n in range(4):
-        dwd[:, lanes(n)] = dot(amt[...], gg[:, lanes(n)])
-    dsend[0:128] = dwd[down_other].astype(BF16)
-    dsend[128:160] = dwd[out_other].astype(BF16)
-    d_copy = remote(dsend, drecv, d_ss, d_rs, xn)
-    d_copy.start()
-
-    pass1(1)
-    pass1(2)
-    last1()
-    out[...] = (tmp[...] + tokens[...].astype(F32) + gv[2:3]).astype(BF16)
-    drain_core1()
-    for t in range(4):
-        norm_grads(t, oy)
-        norm_grads(t, y)
-    for t in range(4):
-        y2(t)
+    pass1(0)
 
     nn = normed.reshape(SEQ * TOK, MODEL)
     for n in range(4):
         dwct[0:GRADS, lanes(n)] = dot(gt[...], nn[:, lanes(n)])
     dwct[GRADS:WIDE] = jnp.zeros((WIDE - GRADS, MODEL), F32)
-    dwct[VEC : VEC + 1] = jnp.sum(dgain[...], 0, keepdims=True)
-    dwct[VEC + 1 : VEC + 2] = jnp.sum(dshift[...], 0, keepdims=True)
-    dwct[VEC + 2 : VEC + 3] = jnp.sum(dbout[...], 0, keepdims=True)
+    dwct[VEC : VEC + 1] = jnp.sum(dbout[...], 0, keepdims=True)
     bias_col = jnp.sum(gt[...].astype(F32), 1, keepdims=True)
     bias_cols = jnp.concatenate(
-        [jnp.zeros((32, HD + 3), F32)]
+        [jnp.zeros((32, HD + 1), F32)]
         + [bias_col[32 * n : 32 * (n + 1)] for n in range(14)]
-        + [jnp.zeros((32, 128 - HD - 17), F32)],
+        + [jnp.zeros((32, 128 - HD - 15), F32)],
         1,
     )
     for j in range(2 * SEQ // 4):
@@ -902,8 +894,29 @@
             dws[dev % 2, dev // 2, :, 384:512] = (piece[:, 384:512] + bias_cols).astype(BF16)
     dx_copy = remote(dws.at[ob], xrecv, dx_ss, dx_rs, xn)
     dx_copy.start()
-    pass2(0)
-    pass2(1)
+
+    for t in range(4):
+        norm_grads(t, oy)
+    for t in range(4):
+        y2(t)
+    pass1(1)
+    for t in range(4):
+        norm_grads(t, y)
+    vsend[0:1] = jnp.sum(dgain[...], 0, keepdims=True)
+    vsend[1:2] = jnp.sum(dshift[...], 0, keepdims=True)
+    vsend[2:8] = jnp.zeros((6, MODEL), F32)
+    vx_copy = remote(vsend, vrecv, vx_ss, vx_rs, xn)
+    vx_copy.start()
+
+    gg = g.reshape(SEQ * TOK, MODEL)
+    for n in range(4):
+        dwd[:, lanes(n)] = dot(amt[...], gg[:, lanes(n)])
+    dsend[0:128] = dwd[down_other].astype(BF16)
+    dsend[128:160] = dwd[out_other].astype(BF16)
+    d_copy = remote(dsend, drecv, d_ss, d_rs, xn)
+    d_copy.start()
+
+    pass1(2)
     dx_copy.wait_recv()
     dws[b] = (dws[b].astype(F32) + xrecv[...].astype(F32)).astype(BF16)
 
@@ -915,24 +928,82 @@
     for off in offsets:
         a_copy(s, shifted(off, 1)).start()
     arecv[s] = dws[b, s]
+    last1()
+    out[...] = (tmp[...] + tokens[...].astype(F32) + gv[2:3]).astype(BF16)
+
+    vx_copy.wait()
+    vrecv[...] += vsend[...]
+
+    def v_copy(source, target):
+        piece = pl.ds(pl.multiple_of(128 * (target // 2), 128), 128)
+        return remote(
+            vrecv.at[:, piece], vparts.at[source], v_ss.at[target], v_rs.at[source], (target, b)
+        )
+
+    for off in offsets:
+        v_copy(s, shifted(off, 1)).start()
+    vparts[s] = vrecv[:, pl.ds(pl.multiple_of(128 * (s // 2), 128), 128)]
+    pass2(0)
     d_copy.wait_recv()
-    d_down[...] = dwd[down_own] + drecv[0:128].astype(F32)
-    d_out[...] = dwd[out_own] + drecv[128:160].astype(F32)
+    d_rows[0:128] = dwd[down_own] + drecv[0:128].astype(F32)
+    d_rows[128:160] = dwd[out_own] + drecv[128:160].astype(F32)
+    norm_gain[...] = gv[...]
+    pass2(1)
     pass2(2)
+    for off in offsets:
+        v_copy(shifted(off, -1), s).wait_recv()
+    ln_sums[...] = jnp.sum(vparts[...], 0)
     last2()
-
+    gn_sum[...] = tmp[...]
+    for off in offsets:
+        a_copy(shifted(off, -1), s).wait_recv()
+
+    for off in offsets:
+        w_copy(s, shifted(off, 1)).wait_send()
+        a_copy(s, shifted(off, 1)).wait_send()
+        v_copy(s, shifted(off, 1)).wait_send()
+    for t in range(SEQ):
+        x_copy(t, b).wait_send()
+    tok_drain()
+    g_drain()
+    drain_core1()
+    drain1()
+    drain_core2()
+    drain2()
+    d_copy.wait_send()
+    dx_copy.wait_send()
+
+
+def finish(
+    tokens_h, cot_h, out_h, gn_sum_h, norm_gain_h, d_rows_h, arecv_h, ln_sums_h,
+    out, d_tok, d_gain, d_shift, d_qkv, d_bqkv, d_out, d_up, d_bup, d_down, d_bout,
+    tokens, cot, gn_sum, norm_gain, d_rows, arecv, ln_sums, sems,
+):
+    moves = [
+        pltpu.make_async_copy(src, dst, sems.at[n])
+        for n, (src, dst) in enumerate(
+            [
+                (gn_sum_h, gn_sum), (tokens_h, tokens), (norm_gain_h, norm_gain), (cot_h, cot),
+                (arecv_h, arecv), (d_rows_h, d_rows), (ln_sums_h, ln_sums), (out_h, out),
+            ]
+        )
+    ]
+    for move in moves:
+        move.start()
+    for move in moves:
+        move.wait()
+    s = lax.axis_index("seq")
+    b = lax.axis_index("batch")
     x = tokens[...].astype(F32)
     centered = x - jnp.mean(x, -1, keepdims=True)
     inv = lax.rsqrt(jnp.mean(centered * centered, -1, keepdims=True) + eps_norm)
     u = centered * inv
-    gu = tmp[...] * gv[0:1]
+    gu = gn_sum[...] * norm_gain[0:1]
     d_tok[...] = cot[...].astype(F32) + inv * (
         gu - jnp.mean(gu, -1, keepdims=True) - u * jnp.mean(gu * u, -1, keepdims=True)
     )
-
-    for off in offsets:
-        a_copy(shifted(off, -1), s).wait_recv()
-    sums = jnp.zeros((32, 128), F32)
+    d_down[...] = d_rows[0:128]
+    d_out[...] = d_rows[128:160]
     for t in range(0, SEQ, 2):
         even, odd = arecv[t].astype(F32), arecv[t + 1].astype(F32)
         d_up[:, UP * t : UP * (t + 1)] = even[:, 0:UP]
@@ -942,40 +1013,31 @@
             d_qkv[:, MODEL * which + HD * t : MODEL * which + HD * (t + 2)] = jnp.concatenate(
                 [even[:, lo : lo + HD], odd[:, lo : lo + HD]], 1
             )
-        sums = sums + even[:, 384:512] + odd[:, 384:512]
-    mine = arecv[s][:, 384:512].astype(F32)
-    picked = [sums[:, HD : HD + 1], sums[:, HD + 1 : HD + 2], mine[:, HD + 2 : HD + 3]]
+    lane_of = lax.broadcasted_iota(jnp.int32, (32, 128), 1)
 
     def pick(block, lane):
         return jnp.sum(jnp.where(lane_of == lane, block, 0.0), 1, keepdims=True)
 
+    mine = arecv[s][:, 384:512].astype(F32)
+    picked = [mine[:, HD : HD + 1]]
     for i in range(4):
-        picked.append(pick(mine, HD + 3 + 4 * b + i))
+        picked.append(pick(mine, HD + 1 + 4 * b + i))
     for i in range(3):
         chunk = 3 * (2 * s + b) + i
         block = arecv[lax.rem(chunk, 32) // 2][:, 384:512].astype(F32)
-        picked.append(pick(block, HD + 3 + 8 + 2 * (chunk // 32) + lax.rem(chunk, 2)))
-    d_vec[...] = jnp.concatenate(picked + [jnp.zeros((32, 118), F32)], 1)
-
-    for off in offsets:
-        w_copy(s, shifted(off, 1)).wait_send()
-        a_copy(s, shifted(off, 1)).wait_send()
-    for t in range(SEQ):
-        x_copy(t, b).wait_send()
-    tok_drain()
-    g_drain()
-    drain1()
-    drain_core2()
-    drain2()
-    d_copy.wait_send()
-    dx_copy.wait_send()
+        picked.append(pick(block, HD + 1 + 8 + 2 * (chunk // 32) + lax.rem(chunk, 2)))
+    rows = jnp.concatenate(picked + [jnp.zeros((32, 120), F32)], 1).T
+    d_bout[...] = rows[0:1]
+    d_bup[...] = jnp.concatenate([rows[1 + i : 2 + i] for i in range(4)], 1)
+    d_bqkv[...] = jnp.concatenate([rows[5 + i : 6 + i] for i in range(3)], 1)
+    turned = pltpu.roll(ln_sums[...], lax.rem(128 - 32 * lax.rem(2 * s + b, 4), 128), 1)
+    d_gain[...] = turned[0:1, 0:32]
+    d_shift[...] = turned[1:2, 0:32]
 
 
 def fast_local(
     tokens, ln_gain, ln_bias, w_qkv, b_qkv, w_out, w_up, b_up, w_down, b_out, cotangent
 ):
-    vec = jnp.concatenate([ln_gain, ln_bias, b_out, b_up, b_qkv]).reshape(10, 32).T
-    vec = jnp.pad(vec, ((0, 0), (0, HD - 10)))
     length = SEQ * TOK
     frequency = rotary_base ** (-(2.0 * np.arange(8)) / 16.0)
     angles = frequency.astype(np.float32)[:, None] * np.arange(length, dtype=np.float32)[None]
@@ -999,14 +1061,13 @@
         out_shape=[
             shape((TOK, MODEL), BF16),
             shape((TOK, MODEL), F32),
-            shape((32, 3 * MODEL), F32),
-            shape((32, MODEL), F32),
-            shape((32, 4 * MODEL), F32),
-            shape((128, MODEL), F32),
-            shape((32, 128), F32),
+            shape((8, MODEL), F32),
+            shape((160, MODEL), F32),
+            shape((SEQ, 32, WIDE), BF16),
+            shape((8, 128), F32),
         ],
-        in_specs=[vm] * 9,
-        out_specs=[vm] * 7,
+        in_specs=[vm] * 13,
+        out_specs=[vm] * 6,
         scratch_shapes=[
             pltpu.VMEM((SEQ, TOK, MODEL), BF16),
             pltpu.VMEM((SEQ, TOK, MODEL), BF16),
@@ -1026,7 +1087,7 @@
             pltpu.VMEM((CHIPS, BT, HD), BF16),
             pltpu.VMEM((CHIPS, BT, HD), BF16),
             pltpu.VMEM((CHIPS, BT, BT), F32),
-            pltpu.VMEM((36, BT, BT), BF16),
+            pltpu.VMEM((18, TOK, MODEL), BF16),
             pltpu.VMEM((1, length), F32),
             pltpu.VMEM((HD, length), F32),
             pltpu.VMEM((GRADS, length), BF16),
@@ -1049,34 +1110,69 @@
             pltpu.VMEM((160, MODEL), BF16),
             pltpu.VMEM((2, SEQ, 32, WIDE), BF16),
             pltpu.VMEM((SEQ, 32, WIDE), BF16),
-            pltpu.VMEM((SEQ, 32, WIDE), BF16),
+            pltpu.VMEM((8, MODEL), F32),
+            pltpu.VMEM((8, MODEL), F32),
+            pltpu.VMEM((SEQ, 8, 128), F32),
             dma((SEQ,)), dma((SEQ,)), dma((SEQ,)), dma((SEQ,)), dma((2,)), dma((2,)),
             dma((4, SEQ)), dma((SEQ,)), dma((4, SEQ)), dma((SEQ,)),
         ]
         + reduce_sems
         + reduce_sems
-        + [dma, dma, dma, dma, dma((SEQ,)), dma((SEQ,))],
+        + [dma, dma, dma, dma, dma((SEQ,)), dma((SEQ,)), dma, dma, dma((SEQ,)), dma((SEQ,))],
         compiler_params=pltpu.CompilerParams(
             collective_id=0, has_side_effects=True, vmem_limit_bytes=62 * 2**20
         ),
     )(
         tokens.reshape(TOK, MODEL), cotangent.reshape(TOK, MODEL),
-        w_qkv, w_out, w_up, w_down, vec, cost, sint,
-    )
-    out, d_tok, d_qkv, d_out, d_up, d_down, d_vec = results
-    vectors = d_vec[:, 0:10].T
+        w_qkv, w_out, w_up, w_down,
+        ln_gain.reshape(1, 32), ln_bias.reshape(1, 32), b_out.reshape(1, 32),
+        b_up.reshape(1, 128), b_qkv.reshape(1, 96), cost, sint,
+    )
+    out, gn_sum, norm_gain, d_rows, arecv, ln_sums = results
+    (out, d_tok, d_gain, d_shift, d_qkv, d_bqkv, d_out, d_up, d_bup, d_down, d_bout) = pl.pallas_call(
+        finish,
+        out_shape=[
+            shape((TOK, MODEL), BF16),
+            shape((TOK, MODEL), F32),
+            shape((1, 32), F32),
+            shape((1, 32), F32),
+            shape((32, 3 * MODEL), F32),
+            shape((1, 96), F32),
+            shape((32, MODEL), F32),
+            shape((32, 4 * MODEL), F32),
+            shape((1, 128), F32),
+            shape((128, MODEL), F32),
+            shape((1, 32), F32),
+        ],
+        in_specs=[pl.BlockSpec(memory_space=pl.ANY)] * 8,
+        out_specs=[vm] * 11,
+        scratch_shapes=[
+            pltpu.VMEM((TOK, MODEL), BF16),
+            pltpu.VMEM((TOK, MODEL), BF16),
+            pltpu.VMEM((TOK, MODEL), F32),
+            pltpu.VMEM((8, MODEL), F32),
+            pltpu.VMEM((160, MODEL), F32),
+            pltpu.VMEM((SEQ, 32, WIDE), BF16),
+            pltpu.VMEM((8, 128), F32),
+            dma((8,)),
+        ],
+        compiler_params=pltpu.CompilerParams(vmem_limit_bytes=62 * 2**20),
+    )(
+        tokens.reshape(TOK, MODEL), cotangent.reshape(TOK, MODEL),
+        out, gn_sum, norm_gain, d_rows, arecv, ln_sums,
+    )
     return (
         out.reshape(tokens.shape),
         d_tok.reshape(tokens.shape),
-        vectors[0],
-        vectors[1],
+        d_gain.reshape(32),
+        d_shift.reshape(32),
         d_qkv,
-        vectors[7:10].reshape(96),
+        d_bqkv.reshape(96),
         d_out,
         d_up,
-        vectors[3:7].reshape(128),
+        d_bup.reshape(128),
         d_down,
-        vectors[2],
+        d_bout.reshape(32),
     )
 
 

time: 164 us -> 140 us (0.85)
  local copies, waits for them, and re-layouts: 13.8 us -> 0 us
  Pallas kernels: 149 us -> 139 us
    pallas_call x1, Pallas kernels: 149 us -> 136 us  [fast_local(): pl.pallas_call(fused, out_shape=[shape((TOK, MODEL), BF16), shape((TOK, M...]
    unnamed x16 -> x0, local copies, waits for them, and re-layouts: 6.53 us -> none
    pallas_call x0 -> x1, Pallas kernels: none -> 3.57 us  [fast_local(): pl.pallas_call(finish, out_shape=[shape((TOK, MODEL), BF16), shape((TOK,...]
    concatenate x1 -> x0, local copies, waits for them, and re-layouts: 3.43 us -> none  [fast_local(): jnp.concatenate([ln_gain, ln_bias, b_out, b_up, b_qkv]).reshape(10, 32)]
where the time goes in v2:
time: 140 us
  Pallas kernels  139 us (99%)
    pallas_call x1, Pallas kernels, fast_local(): pl.pallas_call(fused, out_shape=[shape((TOK, MODEL), BF16), shape((TOK, M...  136 us
    pallas_call x1, Pallas kernels, fast_local(): pl.pallas_call(finish, out_shape=[shape((TOK, MODEL), BF16), shape((TOK,...  3.57 us

profile of v2, /device:TPU:0, one launch (start us, length us, event | category | flops | bytes accessed | tf_op | source)
XLA Modules:
  0.0 140.0 jit_solution(3706850445242159359)
XLA Ops:
  0.6 135.6 %shard_map.212 = (bf16[128,1024]{1,0:T(8,128)(2,1)}, f32[128,1024]{1,0:T(8,128)}, f32[8,1024]{1,0:T(8,128)}, f32[160,1024]{1,0:T(8,128)}, bf16[16,32,512]{2,1,0:T(8,128)(2,1)}, /*index=5*/f32[8,128]{1,0:T(8,128)}) custom-call(bf16[128,1024]{1,0:T(8,128)(2,1)} %bitcast.14, bf16[128,1024]{1,0:T(8,128)(2,1)} %bitcast.16, bf16[32,3072]{1,0:T(8,128)(2,1)} %w_qkv.1, ...), custom_call_target="tpu_custom_call" | custom-call | tf_op jit(solution)/shard_map/pallas_call | solution.py:1059
  136.3 3.6 %shard_map.213 = (bf16[128,1024]{1,0:T(8,128)(2,1)}, f32[128,1024]{1,0:T(8,128)}, f32[1,32]{1,0:T(1,128)}, f32[1,32]{1,0:T(1,128)}, f32[32,3072]{1,0:T(8,128)}, ...) custom-call(bf16[128,1024]{1,0:T(8,128)(2,1)} %bitcast.15, ...), custom_call_target="tpu_custom_call" | custom-call | tf_op jit(solution)/shard_map/pallas_call | solution.py:1132

commit v3 on v2

--- a/solution.py
+++ b/solution.py
@@ -447,6 +447,24 @@
 
     high = z // 2
     zo = [z, z + 1 - 2 * lax.rem(z, 2), 2 - high, 3 - 3 * high]
+    inner = jnp.logical_and(z > 0, z < 3)
+    outer = jnp.logical_or(z == 0, z == 3)
+
+    def mid(*steps):
+        @pl.when(inner)
+        def _():
+            for step in steps:
+                step[0](*step[1:])
+
+    def end(*steps):
+        @pl.when(outer)
+        def _():
+            for step in steps:
+                step[0](*step[1:])
+
+    def both(*steps):
+        for step in steps:
+            step[0](*step[1:])
 
     barrier = pltpu.get_barrier_semaphore()
     for off in offsets:
@@ -505,7 +523,7 @@
         def arrived(shard):
             send(shard, 0, sib).wait_recv()
 
-        def own(act):
+        def on_own_z(act):
             @pl.when(z < 3)
             def _():
                 act(send(s, 0, zp))
@@ -514,8 +532,15 @@
             def _():
                 act(send(s, 1, zm))
 
+        def on_own_y(act):
             act(send(s, 2, yn))
             act(send(s, 3, sib))
+
+        def own_z():
+            on_own_z(start)
+
+        def own_y():
+            on_own_y(start)
 
         def on_z(t, act):
             shard = 4 * zo[t] + 2 * y + c
@@ -549,32 +574,41 @@
             arrived(4 * zo[t] + 2 * row + oc)
 
         def drain():
-            own(finish)
+            on_own_z(finish)
+            on_own_y(finish)
             for t in range(1, 4):
                 on_z(t, finish)
             for t in range(4):
                 on_y(t, finish)
 
-        return (lambda: own(start)), step_z, step_y, step_core, drain
-
-    tok_own, tok_z, tok_y, tok_core, tok_drain = gather(tok, t_ss, t_rs)
-    g_own, g_z, g_y, g_core, g_drain = gather(g, g_ss, g_rs)
-
-    tok_own()
-    for off in offsets:
-        w_copy(s, shifted(off, 1)).start()
+        return own_z, own_y, step_z, step_y, step_core, drain
+
+    tok_oz, tok_oy, tok_z, tok_y, tok_core, tok_drain = gather(tok, t_ss, t_rs)
+    g_oz, g_oy, g_z, g_y, g_core, g_drain = gather(g, g_ss, g_rs)
+
+    def w_send():
+        for off in offsets:
+            w_copy(s, shifted(off, 1)).start()
+
+    def w_arrive(lo, hi):
+        for off in offsets[lo:hi]:
+            source = shifted(off, -1)
+            w_copy(source, s).wait_recv()
+            x_copy(source, b).start()
+
+    both((tok_oz,), (tok_oy,))
+    for off in offsets: w_copy(s, shifted(off, 1)).start()
     x_copy(s, b).start()
-    tok_z(1)
-    tok_y(0)
-    for off in offsets:
-        source = shifted(off, -1)
-        w_copy(source, s).wait_recv()
-        x_copy(source, b).start()
-    for copy in wd_copies:
-        copy.start()
-    for t in range(SEQ):
-        x_copy(t, ob).wait_recv()
-
+    mid((tok_z, 1), (tok_z, 2), (tok_y, 0))
+    end((tok_z, 1), (tok_y, 0))
+    both((g_oy,))
+    end((g_oz,))
+    both((w_arrive, 0, 7))
+    both((w_arrive, 7, 15))
+    mid((tok_z, 3), (g_oz,), (tok_y, 1))
+    end((tok_z, 2), (tok_y, 1))
+    for copy in wd_copies: copy.start()
+    for t in range(SEQ): x_copy(t, ob).wait_recv()
     wct[...] = wc[...].reshape(MODEL, WIDE).T
     rows = wct[VEC : VEC + 16, :].astype(F32)
     gv[0:1] = rows[0:1]
@@ -620,17 +654,22 @@
     def chip_of(t, row):
         return 2 * zo[t] + row
 
-    for t in range(4):
-        tok_core(t, y)
-        project(chip_of(t, y))
-        if t + 2 < 4:
-            tok_z(t + 2)
-        if t == 1:
-            g_own()
-        tok_core(t, oy)
-        project(chip_of(t, oy))
-        if t + 1 < 4:
-            tok_y(t + 1)
+    def proj(t, row):
+        tok_core(t, row)
+        project(chip_of(t, row))
+
+    both((proj, 0, y), (proj, 0, oy), (proj, 1, y))
+    both((proj, 1, oy))
+    end((tok_z, 3), (g_y, 0))
+    mid((g_z, 1), (g_y, 0), (tok_y, 2))
+    both((proj, 2, y))
+    mid((g_z, 2))
+    end((tok_y, 2))
+    both((proj, 2, oy))
+    both((proj, 3, y))
+    end((g_z, 1))
+    both((tok_y, 3), (proj, 3, oy))
+    mid((g_z, 3))
 
     def e_put(n, block):
         m, at = 2 * (n // 4), 256 * (n % 4)
@@ -826,113 +865,102 @@
     dgain[...] = jnp.zeros_like(dgain)
     dshift[...] = jnp.zeros_like(dshift)
     dbout[...] = jnp.zeros_like(dbout)
-    for copy in wd_copies:
-        copy.wait_send()
-    remote(w_down, wd.at[down_other], wd_ss.at[0], wd_rs.at[0], xn).wait_recv()
-    remote(w_out, wd.at[out_other], wd_ss.at[1], wd_rs.at[1], xn).wait_recv()
-
-    g_z(1)
-    g_y(0)
-    for qb in range(CHIPS):
-        attend_fwd(qb)
-    g_z(2)
-    g_core(0, y)
-    grads_at(chip_of(0, y))
-    out_block(0, oy)
-    out_block(0, y)
-    out_block(1, oy)
-    out_block(1, y)
-    g_y(1)
-    g_core(0, oy)
-    grads_at(chip_of(0, oy))
-    g_core(1, y)
-    grads_at(chip_of(1, y))
-    out_block(2, oy)
-    out_block(2, y)
-    out_block(3, oy)
-    out_block(3, y)
-    g_z(3)
-    for t in range(4):
-        y1(t)
-    g_core(1, oy)
-    grads_at(chip_of(1, oy))
-    g_core(2, y)
-    grads_at(chip_of(2, y))
-    g_y(2)
-    g_core(2, oy)
-    grads_at(chip_of(2, oy))
-    g_core(3, y)
-    grads_at(chip_of(3, y))
-    g_y(3)
-    g_core(3, oy)
-    grads_at(chip_of(3, oy))
-
-    for qb in range(CHIPS):
-        attend_bwd(qb)
-    gt[320:384, :] = turn(dkt[...], cost[...], -sint[...]).astype(BF16)
-    gt[384:448, :] = dvt[...].astype(BF16)
-    pass1(0)
-
-    nn = normed.reshape(SEQ * TOK, MODEL)
-    for n in range(4):
-        dwct[0:GRADS, lanes(n)] = dot(gt[...], nn[:, lanes(n)])
-    dwct[GRADS:WIDE] = jnp.zeros((WIDE - GRADS, MODEL), F32)
-    dwct[VEC : VEC + 1] = jnp.sum(dbout[...], 0, keepdims=True)
-    bias_col = jnp.sum(gt[...].astype(F32), 1, keepdims=True)
-    bias_cols = jnp.concatenate(
-        [jnp.zeros((32, HD + 1), F32)]
-        + [bias_col[32 * n : 32 * (n + 1)] for n in range(14)]
-        + [jnp.zeros((32, 128 - HD - 15), F32)],
-        1,
-    )
-    for j in range(2 * SEQ // 4):
-        turned = dwct[:, 128 * j : 128 * (j + 1)].T
-        for i in range(4):
-            piece = turned[32 * i : 32 * (i + 1)]
-            dev = 4 * j + i
-            dws[dev % 2, dev // 2, :, 0:384] = piece[:, 0:384].astype(BF16)
-            dws[dev % 2, dev // 2, :, 384:512] = (piece[:, 384:512] + bias_cols).astype(BF16)
-    dx_copy = remote(dws.at[ob], xrecv, dx_ss, dx_rs, xn)
-    dx_copy.start()
-
-    for t in range(4):
-        norm_grads(t, oy)
-    for t in range(4):
-        y2(t)
-    pass1(1)
-    for t in range(4):
-        norm_grads(t, y)
-    vsend[0:1] = jnp.sum(dgain[...], 0, keepdims=True)
-    vsend[1:2] = jnp.sum(dshift[...], 0, keepdims=True)
-    vsend[2:8] = jnp.zeros((6, MODEL), F32)
+
+    def wd_arrive():
+        for copy in wd_copies:
+            copy.wait_send()
+        remote(w_down, wd.at[down_other], wd_ss.at[0], wd_rs.at[0], xn).wait_recv()
+        remote(w_out, wd.at[out_other], wd_ss.at[1], wd_rs.at[1], xn).wait_recv()
+
+    def fwd(lo, hi):
+        for qb in range(lo, hi):
+            attend_fwd(qb)
+
+    def grads(t, row):
+        g_core(t, row)
+        grads_at(chip_of(t, row))
+
+    def bwd(lo, hi):
+        for qb in range(lo, hi):
+            attend_bwd(qb)
+
+    def bwd_keys():
+        gt[320:384, :] = turn(dkt[...], cost[...], -sint[...]).astype(BF16)
+        gt[384:448, :] = dvt[...].astype(BF16)
+
+    dx_copies = [remote(dws.at[p, ob], xrecv.at[p], dx_ss.at[p], dx_rs.at[p], xn) for p in range(2)]
+
+    def turn_out(p, extra):
+        for j in range(2 * SEQ // 4):
+            turned = dwct[256 * p : 256 * (p + 1), 128 * j : 128 * (j + 1)].T
+            for i in range(4):
+                piece = turned[32 * i : 32 * (i + 1)]
+                dev = 4 * j + i
+                at = dws.at[p, dev % 2, dev // 2]
+                if extra is None:
+                    at[...] = piece.astype(BF16)
+                else:
+                    at[:, 0:128] = piece[:, 0:128].astype(BF16)
+                    at[:, 128:256] = (piece[:, 128:256] + extra).astype(BF16)
+        dx_copies[p].start()
+
+    def up_grads():
+        nn = normed.reshape(SEQ * TOK, MODEL)
+        for n in range(4):
+            dwct[0:256, lanes(n)] = dot(gt[0:256], nn[:, lanes(n)])
+        turn_out(0, None)
+
+    def qkv_grads():
+        nn = normed.reshape(SEQ * TOK, MODEL)
+        for n in range(4):
+            dwct[256:GRADS, lanes(n)] = dot(gt[256:GRADS], nn[:, lanes(n)])
+        dwct[GRADS:WIDE] = jnp.zeros((WIDE - GRADS, MODEL), F32)
+        dwct[VEC : VEC + 1] = jnp.sum(dbout[...], 0, keepdims=True)
+        bias_col = jnp.sum(gt[...].astype(F32), 1, keepdims=True)
+        turn_out(
+            1,
+            jnp.concatenate(
+                [jnp.zeros((32, HD + 1), F32)]
+                + [bias_col[32 * n : 32 * (n + 1)] for n in range(14)]
+                + [jnp.zeros((32, 128 - HD - 15), F32)],
+                1,
+            ),
+        )
+
     vx_copy = remote(vsend, vrecv, vx_ss, vx_rs, xn)
-    vx_copy.start()
-
-    gg = g.reshape(SEQ * TOK, MODEL)
-    for n in range(4):
-        dwd[:, lanes(n)] = dot(amt[...], gg[:, lanes(n)])
-    dsend[0:128] = dwd[down_other].astype(BF16)
-    dsend[128:160] = dwd[out_other].astype(BF16)
+
+    def ln_grads():
+        vsend[0:1] = jnp.sum(dgain[...], 0, keepdims=True)
+        vsend[1:2] = jnp.sum(dshift[...], 0, keepdims=True)
+        vsend[2:8] = jnp.zeros((6, MODEL), F32)
+        vx_copy.start()
+
     d_copy = remote(dsend, drecv, d_ss, d_rs, xn)
-    d_copy.start()
-
-    pass1(2)
-    dx_copy.wait_recv()
-    dws[b] = (dws[b].astype(F32) + xrecv[...].astype(F32)).astype(BF16)
-
-    def a_copy(source, target):
+
+    def down_grads():
+        gg = g.reshape(SEQ * TOK, MODEL)
+        for n in range(4):
+            dwd[:, lanes(n)] = dot(amt[...], gg[:, lanes(n)])
+        dsend[0:128] = dwd[down_other].astype(BF16)
+        dsend[128:160] = dwd[out_other].astype(BF16)
+        d_copy.start()
+
+    def a_copy(p, source, target):
         return remote(
-            dws.at[b, target], arecv.at[source], a_ss.at[target], a_rs.at[source], (target, b)
-        )
-
-    for off in offsets:
-        a_copy(s, shifted(off, 1)).start()
-    arecv[s] = dws[b, s]
-    last1()
-    out[...] = (tmp[...] + tokens[...].astype(F32) + gv[2:3]).astype(BF16)
-
-    vx_copy.wait()
-    vrecv[...] += vsend[...]
+            dws.at[p, b, target], arecv.at[p, source], a_ss.at[p, target], a_rs.at[p, source],
+            (target, b),
+        )
+
+    def wide_out(p):
+        dx_copies[p].wait_recv()
+        dws[p, b] = (dws[p, b].astype(F32) + xrecv[p].astype(F32)).astype(BF16)
+        for off in offsets:
+            a_copy(p, s, shifted(off, 1)).start()
+        arecv[p, s] = dws[p, b, s]
+
+    def end1():
+        last1()
+        out[...] = (tmp[...] + tokens[...].astype(F32) + gv[2:3]).astype(BF16)
 
     def v_copy(source, target):
         piece = pl.ds(pl.multiple_of(128 * (target // 2), 128), 128)
@@ -940,27 +968,67 @@
             vrecv.at[:, piece], vparts.at[source], v_ss.at[target], v_rs.at[source], (target, b)
         )
 
-    for off in offsets:
-        v_copy(s, shifted(off, 1)).start()
-    vparts[s] = vrecv[:, pl.ds(pl.multiple_of(128 * (s // 2), 128), 128)]
-    pass2(0)
-    d_copy.wait_recv()
-    d_rows[0:128] = dwd[down_own] + drecv[0:128].astype(F32)
-    d_rows[128:160] = dwd[out_own] + drecv[128:160].astype(F32)
-    norm_gain[...] = gv[...]
-    pass2(1)
-    pass2(2)
-    for off in offsets:
-        v_copy(shifted(off, -1), s).wait_recv()
-    ln_sums[...] = jnp.sum(vparts[...], 0)
-    last2()
-    gn_sum[...] = tmp[...]
-    for off in offsets:
-        a_copy(shifted(off, -1), s).wait_recv()
+    def ln_out():
+        vx_copy.wait()
+        vrecv[...] += vsend[...]
+        for off in offsets:
+            v_copy(s, shifted(off, 1)).start()
+        vparts[s] = vrecv[:, pl.ds(pl.multiple_of(128 * (s // 2), 128), 128)]
+
+    def down_out():
+        d_copy.wait_recv()
+        d_rows[0:128] = dwd[down_own] + drecv[0:128].astype(F32)
+        d_rows[128:160] = dwd[out_own] + drecv[128:160].astype(F32)
+        norm_gain[...] = gv[...]
+
+    def ln_arrive():
+        for off in offsets:
+            v_copy(shifted(off, -1), s).wait_recv()
+        ln_sums[...] = jnp.sum(vparts[...], 0)
+
+    def end2():
+        last2()
+        gn_sum[...] = tmp[...]
+
+    def wide_arrive():
+        for off in offsets:
+            a_copy(0, shifted(off, -1), s).wait_recv()
+            a_copy(1, shifted(off, -1), s).wait_recv()
+
+    both((wd_arrive,), (fwd, 0, 5))
+    mid((g_y, 1))
+    end((g_z, 2))
+    both((fwd, 5, 8))
+    end((g_y, 1))
+    both((grads, 0, y), (out_block, 0, oy), (out_block, 1, oy), (out_block, 2, oy), (out_block, 3, oy))
+    end((g_z, 3))
+    both((y1, 0), (y1, 1), (y1, 2), (y1, 3))
+    both((out_block, 0, y), (out_block, 1, y), (out_block, 2, y), (out_block, 3, y))
+    both((grads, 0, oy), (grads, 1, y), (grads, 1, oy), (grads, 2, y), (g_y, 2), (grads, 2, oy), (grads, 3, y))
+    both((g_y, 3), (grads, 3, oy))
+    both((up_grads,))
+    end((pass1, 0))
+    both((bwd, 0, 8), (bwd_keys,))
+    end((pass1, 1))
+    both((qkv_grads,))
+    both((wide_out, 0))
+    both((norm_grads, 0, oy), (norm_grads, 1, oy), (norm_grads, 2, oy), (norm_grads, 3, oy))
+    both((y2, 0), (y2, 1), (y2, 2), (y2, 3))
+    end((pass1, 2))
+    mid((pass1, 0))
+    both((norm_grads, 0, y), (norm_grads, 1, y), (norm_grads, 2, y), (norm_grads, 3, y))
+    mid((pass1, 1), (pass1, 2))
+    both((ln_grads,), (down_grads,))
+    both((wide_out, 1))
+    both((end1,), (ln_out,), (pass2, 0))
+    both((pass2, 1))
+    both((down_out,))
+    both((pass2, 2), (ln_arrive,), (end2,), (wide_arrive,))
 
     for off in offsets:
         w_copy(s, shifted(off, 1)).wait_send()
-        a_copy(s, shifted(off, 1)).wait_send()
+        a_copy(0, s, shifted(off, 1)).wait_send()
+        a_copy(1, s, shifted(off, 1)).wait_send()
         v_copy(s, shifted(off, 1)).wait_send()
     for t in range(SEQ):
         x_copy(t, b).wait_send()
@@ -971,7 +1039,8 @@
     drain_core2()
     drain2()
     d_copy.wait_send()
-    dx_copy.wait_send()
+    for copy in dx_copies:
+        copy.wait_send()
 
 
 def finish(
@@ -1005,11 +1074,11 @@
     d_down[...] = d_rows[0:128]
     d_out[...] = d_rows[128:160]
     for t in range(0, SEQ, 2):
-        even, odd = arecv[t].astype(F32), arecv[t + 1].astype(F32)
-        d_up[:, UP * t : UP * (t + 1)] = even[:, 0:UP]
-        d_up[:, UP * (t + 1) : UP * (t + 2)] = odd[:, 0:UP]
+        even, odd = arecv[1, t].astype(F32), arecv[1, t + 1].astype(F32)
+        d_up[:, UP * t : UP * (t + 1)] = arecv[0, t].astype(F32)
+        d_up[:, UP * (t + 1) : UP * (t + 2)] = arecv[0, t + 1].astype(F32)
         for which in range(3):
-            lo = UP + HD * which
+            lo = HD * which
             d_qkv[:, MODEL * which + HD * t : MODEL * which + HD * (t + 2)] = jnp.concatenate(
                 [even[:, lo : lo + HD], odd[:, lo : lo + HD]], 1
             )
@@ -1018,13 +1087,13 @@
     def pick(block, lane):
         return jnp.sum(jnp.where(lane_of == lane, block, 0.0), 1, keepdims=True)
 
-    mine = arecv[s][:, 384:512].astype(F32)
+    mine = arecv[1, s][:, 128:256].astype(F32)
     picked = [mine[:, HD : HD + 1]]
     for i in range(4):
         picked.append(pick(mine, HD + 1 + 4 * b + i))
     for i in range(3):
         chunk = 3 * (2 * s + b) + i
-        block = arecv[lax.rem(chunk, 32) // 2][:, 384:512].astype(F32)
+        block = arecv[1, lax.rem(chunk, 32) // 2][:, 128:256].astype(F32)
         picked.append(pick(block, HD + 1 + 8 + 2 * (chunk // 32) + lax.rem(chunk, 2)))
     rows = jnp.concatenate(picked + [jnp.zeros((32, 120), F32)], 1).T
     d_bout[...] = rows[0:1]
@@ -1063,7 +1132,7 @@
             shape((TOK, MODEL), F32),
             shape((8, MODEL), F32),
             shape((160, MODEL), F32),
-            shape((SEQ, 32, WIDE), BF16),
+            shape((2, SEQ, 32, 256), BF16),
             shape((8, 128), F32),
         ],
         in_specs=[vm] * 13,
@@ -1108,8 +1177,8 @@
             pltpu.VMEM((UP + HD, MODEL), F32),
             pltpu.VMEM((160, MODEL), BF16),
             pltpu.VMEM((160, MODEL), BF16),
-            pltpu.VMEM((2, SEQ, 32, WIDE), BF16),
-            pltpu.VMEM((SEQ, 32, WIDE), BF16),
+            pltpu.VMEM((2, 2, SEQ, 32, 256), BF16),
+            pltpu.VMEM((2, SEQ, 32, 256), BF16),
             pltpu.VMEM((8, MODEL), F32),
             pltpu.VMEM((8, MODEL), F32),
             pltpu.VMEM((SEQ, 8, 128), F32),
@@ -1118,7 +1187,7 @@
         ]
         + reduce_sems
         + reduce_sems
-        + [dma, dma, dma, dma, dma((SEQ,)), dma((SEQ,)), dma, dma, dma((SEQ,)), dma((SEQ,))],
+        + [dma, dma, dma((2,)), dma((2,)), dma((2, SEQ)), dma((2, SEQ)), dma, dma, dma((SEQ,)), dma((SEQ,))],
         compiler_params=pltpu.CompilerParams(
             collective_id=0, has_side_effects=True, vmem_limit_bytes=62 * 2**20
         ),
@@ -1152,7 +1221,7 @@
             pltpu.VMEM((TOK, MODEL), F32),
             pltpu.VMEM((8, MODEL), F32),
             pltpu.VMEM((160, MODEL), F32),
-            pltpu.VMEM((SEQ, 32, WIDE), BF16),
+            pltpu.VMEM((2, SEQ, 32, 256), BF16),
             pltpu.VMEM((8, 128), F32),
             dma((8,)),
         ],

time: 140 us -> 124 us (0.89)
  Pallas kernels: 139 us -> 123 us
    pallas_call x1, Pallas kernels: 136 us -> 120 us  [fast_local(): pl.pallas_call(fused, out_shape=[shape((TOK, MODEL), BF16), shape((TOK, M...]
where the time goes in v3:
time: 124 us
  Pallas kernels  123 us (99%)
    pallas_call x1, Pallas kernels, fast_local(): pl.pallas_call(fused, out_shape=[shape((TOK, MODEL), BF16), shape((TOK, M...  120 us
    pallas_call x1, Pallas kernels, fast_local(): pl.pallas_call(finish, out_shape=[shape((TOK, MODEL), BF16), shape((TOK,...  3.57 us

profile of v3, /device:TPU:0, one launch (start us, length us, event | category | flops | bytes accessed | tf_op | source)
XLA Modules:
  0.0 123.9 jit_solution(13637543803476575784)
XLA Ops:
  0.6 119.5 %shard_map.212 = (bf16[128,1024]{1,0:T(8,128)(2,1)}, f32[128,1024]{1,0:T(8,128)}, f32[8,1024]{1,0:T(8,128)}, f32[160,1024]{1,0:T(8,128)}, bf16[2,16,32,256]{3,2,1,0:T(8,128)(2,1)}, /*index=5*/f32[8,128]{1,0:T(8,128)}) custom-call(bf16[128,1024]{1,0:T(8,128)(2,1)} %bitcast.14, bf16[128,1024]{1,0:T(8,128)(2,1)} %bitcast.16, bf16[32,3072]{1,0:T(8,128)(2,1)} %w_qkv.1, ...), custom_call_target="tpu_custom_call" | custom-call | tf_op jit(solution)/shard_map/pallas_call | solution.py:1128
  120.2 3.6 %shard_map.213 = (bf16[128,1024]{1,0:T(8,128)(2,1)}, f32[128,1024]{1,0:T(8,128)}, f32[1,32]{1,0:T(1,128)}, f32[1,32]{1,0:T(1,128)}, f32[32,3072]{1,0:T(8,128)}, ...) custom-call(bf16[128,1024]{1,0:T(8,128)(2,1)} %bitcast.15, ...), custom_call_target="tpu_custom_call" | custom-call | tf_op jit(solution)/shard_map/pallas_call | solution.py:1201

commit v4 on v3

--- a/solution.py
+++ b/solution.py
@@ -416,9 +416,9 @@
 
 
 def fused(
-    tokens, cot, w_qkv, w_out, w_up, w_down, gain, shift, bout, bup, bqkv, cost, sint,
-    out, gn_sum, norm_gain, d_rows, arecv, ln_sums,
-    tok, g, wsend, wc, wct, wd, gv, bct, normed, unit, amt, dactt, qt, kt, vt, k, v, sbuf, e,
+    tokens_h, cot_h, w_qkv_h, w_out_h, w_up_h, w_down_h, gain, shift, bout, bup, bqkv, cost, sint,
+    out_h, gn_sum_h, norm_gain_h, d_rows_h, arecv_h, ln_sums_h,
+    out, d_rows, arecv, ln_sums, res_sems, w_qkv, w_up, in_sems, tok, g, wsend, wc, wct, wd, gv, bct, normed, unit, amt, dactt, qt, kt, vt, k, v, sbuf, e,
     linv, ot, gt, dost, delta, dkt, dvt, part1, rc1, ry1, rzl1, rzr1, rc2, ry2, rzl2, rzr2, tmp,
     dgain, dshift, dbout, dwct, dwd, dsend, drecv, dws, xrecv, vsend, vrecv, vparts,
     w_ss, w_rs, x_ss, x_rs, wd_ss, wd_rs, t_ss, t_rs, g_ss, g_rs,
@@ -473,11 +473,29 @@
         )
     pl.semaphore_signal(barrier, inc=1, device_id=xn, device_id_type=MESH)
 
+    down_own = pl.ds(pl.multiple_of(128 * b, 128), 128)
+    down_other = pl.ds(pl.multiple_of(128 * ob, 128), 128)
+    out_own = pl.ds(pl.multiple_of(UP + 32 * b, 32), 32)
+    out_other = pl.ds(pl.multiple_of(UP + 32 * ob, 32), 32)
+    loads = [
+        pltpu.make_async_copy(src, dst, in_sems.at[n])
+        for n, (src, dst) in enumerate(
+            [
+                (w_up_h, w_up), (w_qkv_h, w_qkv), (tokens_h, tok.at[s]), (cot_h, g.at[s]),
+                (w_down_h, wd.at[down_own]), (w_out_h, wd.at[out_own]),
+            ]
+        )
+    ]
+    for load in loads:
+        load.start()
+
     vectors = [gain[...], shift[...], bout[...]]
     vectors += [bup[:, 32 * i : 32 * (i + 1)] for i in range(4)]
     vectors += [bqkv[:, 32 * i : 32 * (i + 1)] for i in range(3)]
     vec = jnp.concatenate([w.astype(F32) for w in vectors] + [jnp.zeros((6, 32), F32)], 0).T
     vec = jnp.concatenate([vec, jnp.zeros((32, HD - 16), F32)], 1).astype(BF16)
+    loads[0].wait()
+    loads[1].wait()
     for t in range(SEQ):
         wsend[t] = jnp.concatenate(
             [
@@ -490,14 +508,8 @@
             1,
         )
     wc[2 * s + b] = wsend[s]
-    tok[s] = tokens[...]
-    g[s] = cot[...]
-    down_own = pl.ds(pl.multiple_of(128 * b, 128), 128)
-    down_other = pl.ds(pl.multiple_of(128 * ob, 128), 128)
-    out_own = pl.ds(pl.multiple_of(UP + 32 * b, 32), 32)
-    out_other = pl.ds(pl.multiple_of(UP + 32 * ob, 32), 32)
-    wd[down_own] = w_down[...]
-    wd[out_own] = w_out[...]
+    for load in loads[2:6]:
+        load.wait()
     pl.semaphore_wait(barrier, SEQ)
 
     def w_copy(source, target):
@@ -512,8 +524,8 @@
         )
 
     wd_copies = [
-        remote(w_down, wd.at[down_own], wd_ss.at[0], wd_rs.at[0], xn),
-        remote(w_out, wd.at[out_own], wd_ss.at[1], wd_rs.at[1], xn),
+        remote(wd.at[down_own], wd.at[down_own], wd_ss.at[0], wd_rs.at[0], xn),
+        remote(wd.at[out_own], wd.at[out_own], wd_ss.at[1], wd_rs.at[1], xn),
     ]
 
     def gather(buf, ss, rs):
@@ -586,8 +598,8 @@
     tok_oz, tok_oy, tok_z, tok_y, tok_core, tok_drain = gather(tok, t_ss, t_rs)
     g_oz, g_oy, g_z, g_y, g_core, g_drain = gather(g, g_ss, g_rs)
 
-    def w_send():
-        for off in offsets:
+    def w_send(lo, hi):
+        for off in offsets[lo:hi]:
             w_copy(s, shifted(off, 1)).start()
 
     def w_arrive(lo, hi):
@@ -605,12 +617,13 @@
     end((g_oz,))
     both((w_arrive, 0, 7))
     both((w_arrive, 7, 15))
-    mid((tok_z, 3), (g_oz,), (tok_y, 1))
+    mid((tok_z, 3), (tok_y, 1))
     end((tok_z, 2), (tok_y, 1))
     for copy in wd_copies: copy.start()
     for t in range(SEQ): x_copy(t, ob).wait_recv()
     wct[...] = wc[...].reshape(MODEL, WIDE).T
     rows = wct[VEC : VEC + 16, :].astype(F32)
+    gv[...] = jnp.zeros_like(gv)
     gv[0:1] = rows[0:1]
     gv[1:2] = rows[1:2]
     gv[2:3] = rows[2:3]
@@ -658,7 +671,9 @@
         tok_core(t, row)
         project(chip_of(t, row))
 
-    both((proj, 0, y), (proj, 0, oy), (proj, 1, y))
+    both((proj, 0, y))
+    mid((g_oz,))
+    both((proj, 0, oy), (proj, 1, y))
     both((proj, 1, oy))
     end((tok_z, 3), (g_y, 0))
     mid((g_z, 1), (g_y, 0), (tok_y, 2))
@@ -869,8 +884,8 @@
     def wd_arrive():
         for copy in wd_copies:
             copy.wait_send()
-        remote(w_down, wd.at[down_other], wd_ss.at[0], wd_rs.at[0], xn).wait_recv()
-        remote(w_out, wd.at[out_other], wd_ss.at[1], wd_rs.at[1], xn).wait_recv()
+        remote(wd.at[down_other], wd.at[down_other], wd_ss.at[0], wd_rs.at[0], xn).wait_recv()
+        remote(wd.at[out_other], wd.at[out_other], wd_ss.at[1], wd_rs.at[1], xn).wait_recv()
 
     def fwd(lo, hi):
         for qb in range(lo, hi):
@@ -958,9 +973,20 @@
             a_copy(p, s, shifted(off, 1)).start()
         arecv[p, s] = dws[p, b, s]
 
+    res_copies = [
+        pltpu.make_async_copy(src, dst, res_sems.at[n])
+        for n, (src, dst) in enumerate(
+            [
+                (out, out_h), (tmp, gn_sum_h), (gv, norm_gain_h), (d_rows, d_rows_h),
+                (arecv, arecv_h), (ln_sums, ln_sums_h),
+            ]
+        )
+    ]
+
     def end1():
         last1()
-        out[...] = (tmp[...] + tokens[...].astype(F32) + gv[2:3]).astype(BF16)
+        out[...] = (tmp[...] + tok[s].astype(F32) + gv[2:3]).astype(BF16)
+        res_copies[0].start()
 
     def v_copy(source, target):
         piece = pl.ds(pl.multiple_of(128 * (target // 2), 128), 128)
@@ -979,21 +1005,24 @@
         d_copy.wait_recv()
         d_rows[0:128] = dwd[down_own] + drecv[0:128].astype(F32)
         d_rows[128:160] = dwd[out_own] + drecv[128:160].astype(F32)
-        norm_gain[...] = gv[...]
+        res_copies[2].start()
+        res_copies[3].start()
 
     def ln_arrive():
         for off in offsets:
             v_copy(shifted(off, -1), s).wait_recv()
         ln_sums[...] = jnp.sum(vparts[...], 0)
+        res_copies[5].start()
 
     def end2():
         last2()
-        gn_sum[...] = tmp[...]
+        res_copies[1].start()
 
     def wide_arrive():
         for off in offsets:
             a_copy(0, shifted(off, -1), s).wait_recv()
             a_copy(1, shifted(off, -1), s).wait_recv()
+        res_copies[4].start()
 
     both((wd_arrive,), (fwd, 0, 5))
     mid((g_y, 1))
@@ -1020,10 +1049,11 @@
     mid((pass1, 1), (pass1, 2))
     both((ln_grads,), (down_grads,))
     both((wide_out, 1))
-    both((end1,), (ln_out,), (pass2, 0))
+    end((end1,), (pass2, 0), (ln_out,))
+    mid((ln_out,), (end1,), (pass2, 0))
     both((pass2, 1))
     both((down_out,))
-    both((pass2, 2), (ln_arrive,), (end2,), (wide_arrive,))
+    both((pass2, 2), (ln_arrive,), (wide_arrive,), (end2,))
 
     for off in offsets:
         w_copy(s, shifted(off, 1)).wait_send()
@@ -1041,28 +1071,57 @@
     d_copy.wait_send()
     for copy in dx_copies:
         copy.wait_send()
+    for copy in res_copies:
+        copy.wait()
 
 
 def finish(
     tokens_h, cot_h, out_h, gn_sum_h, norm_gain_h, d_rows_h, arecv_h, ln_sums_h,
-    out, d_tok, d_gain, d_shift, d_qkv, d_bqkv, d_out, d_up, d_bup, d_down, d_bout,
-    tokens, cot, gn_sum, norm_gain, d_rows, arecv, ln_sums, sems,
+    out, d_tok_h, d_gain, d_shift, d_qkv_h, d_bqkv, d_out, d_up_h, d_bup, d_down, d_bout,
+    tokens, cot, gn_sum, norm_gain, arecv, ln_sums, d_tok, d_qkv, d_up, kept, rows, sems, out_sems,
 ):
-    moves = [
+    loads = [
         pltpu.make_async_copy(src, dst, sems.at[n])
         for n, (src, dst) in enumerate(
             [
+                (arecv_h.at[0], arecv.at[0]), (arecv_h.at[1], arecv.at[1]),
                 (gn_sum_h, gn_sum), (tokens_h, tokens), (norm_gain_h, norm_gain), (cot_h, cot),
-                (arecv_h, arecv), (d_rows_h, d_rows), (ln_sums_h, ln_sums), (out_h, out),
+                (ln_sums_h, ln_sums), (out_h, kept), (d_rows_h, rows),
             ]
         )
     ]
-    for move in moves:
+    stores = [
+        pltpu.make_async_copy(src, dst, out_sems.at[n])
+        for n, (src, dst) in enumerate(
+            [
+                (kept, out), (rows.at[0:128], d_down), (rows.at[128:160], d_out),
+                (d_up, d_up_h), (d_qkv, d_qkv_h), (d_tok, d_tok_h),
+            ]
+        )
+    ]
+    for move in loads:
         move.start()
-    for move in moves:
-        move.wait()
     s = lax.axis_index("seq")
     b = lax.axis_index("batch")
+    loads[0].wait()
+    for t in range(SEQ):
+        d_up[:, UP * t : UP * (t + 1)] = arecv[0, t].astype(F32)
+    stores[3].start()
+    loads[7].wait()
+    loads[8].wait()
+    for move in stores[0:3]:
+        move.start()
+    loads[1].wait()
+    for t in range(0, SEQ, 2):
+        even, odd = arecv[1, t].astype(F32), arecv[1, t + 1].astype(F32)
+        for which in range(3):
+            lo = HD * which
+            d_qkv[:, MODEL * which + HD * t : MODEL * which + HD * (t + 2)] = jnp.concatenate(
+                [even[:, lo : lo + HD], odd[:, lo : lo + HD]], 1
+            )
+    stores[4].start()
+    for move in loads[2:7]:
+        move.wait()
     x = tokens[...].astype(F32)
     centered = x - jnp.mean(x, -1, keepdims=True)
     inv = lax.rsqrt(jnp.mean(centered * centered, -1, keepdims=True) + eps_norm)
@@ -1071,17 +1130,7 @@
     d_tok[...] = cot[...].astype(F32) + inv * (
         gu - jnp.mean(gu, -1, keepdims=True) - u * jnp.mean(gu * u, -1, keepdims=True)
     )
-    d_down[...] = d_rows[0:128]
-    d_out[...] = d_rows[128:160]
-    for t in range(0, SEQ, 2):
-        even, odd = arecv[1, t].astype(F32), arecv[1, t + 1].astype(F32)
-        d_up[:, UP * t : UP * (t + 1)] = arecv[0, t].astype(F32)
-        d_up[:, UP * (t + 1) : UP * (t + 2)] = arecv[0, t + 1].astype(F32)
-        for which in range(3):
-            lo = HD * which
-            d_qkv[:, MODEL * which + HD * t : MODEL * which + HD * (t + 2)] = jnp.concatenate(
-                [even[:, lo : lo + HD], odd[:, lo : lo + HD]], 1
-            )
+    stores[5].start()
     lane_of = lax.broadcasted_iota(jnp.int32, (32, 128), 1)
 
     def pick(block, lane):
@@ -1102,6 +1151,8 @@
     turned = pltpu.roll(ln_sums[...], lax.rem(128 - 32 * lax.rem(2 * s + b, 4), 128), 1)
     d_gain[...] = turned[0:1, 0:32]
     d_shift[...] = turned[1:2, 0:32]
+    for move in stores:
+        move.wait()
 
 
 def fast_local(
@@ -1113,6 +1164,7 @@
     cost = jnp.asarray(np.cos(angles.astype(np.float64)).astype(np.float32))
     sint = jnp.asarray(np.sin(angles.astype(np.float64)).astype(np.float32))
     vm = pl.BlockSpec(memory_space=pltpu.VMEM)
+    far = pl.BlockSpec(memory_space=pl.ANY)
     shape = jax.ShapeDtypeStruct
     dma = pltpu.SemaphoreType.DMA
 
@@ -1135,9 +1187,17 @@
             shape((2, SEQ, 32, 256), BF16),
             shape((8, 128), F32),
         ],
-        in_specs=[vm] * 13,
-        out_specs=[vm] * 6,
+        in_specs=[far] * 6 + [vm] * 7,
+        out_specs=[far] * 6,
         scratch_shapes=[
+            pltpu.VMEM((TOK, MODEL), BF16),
+            pltpu.VMEM((160, MODEL), F32),
+            pltpu.VMEM((2, SEQ, 32, 256), BF16),
+            pltpu.VMEM((8, 128), F32),
+            dma((6,)),
+            pltpu.VMEM((32, 3 * MODEL), BF16),
+            pltpu.VMEM((32, 4 * MODEL), BF16),
+            dma((6,)),
             pltpu.VMEM((SEQ, TOK, MODEL), BF16),
             pltpu.VMEM((SEQ, TOK, MODEL), BF16),
             pltpu.VMEM((SEQ, 32, WIDE), BF16),
@@ -1213,17 +1273,22 @@
             shape((128, MODEL), F32),
             shape((1, 32), F32),
         ],
-        in_specs=[pl.BlockSpec(memory_space=pl.ANY)] * 8,
-        out_specs=[vm] * 11,
+        in_specs=[far] * 8,
+        out_specs=[far, far, vm, vm, far, vm, far, far, vm, far, vm],
         scratch_shapes=[
             pltpu.VMEM((TOK, MODEL), BF16),
             pltpu.VMEM((TOK, MODEL), BF16),
             pltpu.VMEM((TOK, MODEL), F32),
             pltpu.VMEM((8, MODEL), F32),
-            pltpu.VMEM((160, MODEL), F32),
             pltpu.VMEM((2, SEQ, 32, 256), BF16),
             pltpu.VMEM((8, 128), F32),
-            dma((8,)),
+            pltpu.VMEM((TOK, MODEL), F32),
+            pltpu.VMEM((32, 3 * MODEL), F32),
+            pltpu.VMEM((32, 4 * MODEL), F32),
+            pltpu.VMEM((TOK, MODEL), BF16),
+            pltpu.VMEM((160, MODEL), F32),
+            dma((9,)),
+            dma((6,)),
         ],
         compiler_params=pltpu.CompilerParams(vmem_limit_bytes=62 * 2**20),
     )(

time: 124 us -> 123 us (level)
  no operation moved by 1% of the time
where the time goes in v4:
time: 123 us
  Pallas kernels  122 us (99%)
    pallas_call x1, Pallas kernels, fast_local(): pl.pallas_call(fused, out_shape=[shape((TOK, MODEL), BF16), shape((TOK, M...  118 us
    pallas_call x1, Pallas kernels, fast_local(): pl.pallas_call(finish, out_shape=[shape((TOK, MODEL), BF16), shape((TOK,...  3.65 us

profile of v4, /device:TPU:0, one launch (start us, length us, event | category | flops | bytes accessed | tf_op | source)
XLA Modules:
  0.0 122.8 jit_solution(7088779941303253856)
XLA Ops:
  0.6 118.3 %shard_map.212 = (bf16[128,1024]{1,0:T(8,128)(2,1)}, f32[128,1024]{1,0:T(8,128)}, f32[8,1024]{1,0:T(8,128)}, f32[160,1024]{1,0:T(8,128)}, bf16[2,16,32,256]{3,2,1,0:T(8,128)(2,1)}, /*index=5*/f32[8,128]{1,0:T(8,128)}) custom-call(bf16[128,1024]{1,0:T(8,128)(2,1)} %bitcast.14, bf16[128,1024]{1,0:T(8,128)(2,1)} %bitcast.16, bf16[32,3072]{1,0:T(8,128)(2,1)} %w_qkv_h.1, ...), custom_call_target="tpu_custom_call" | custom-call | tf_op jit(solution)/shard_map/pallas_call | solution.py:1180
  118.9 3.6 %shard_map.213 = (bf16[128,1024]{1,0:T(8,128)(2,1)}, f32[128,1024]{1,0:T(8,128)}, f32[1,32]{1,0:T(1,128)}, f32[1,32]{1,0:T(1,128)}, f32[32,3072]{1,0:T(8,128)}, ...) custom-call(bf16[128,1024]{1,0:T(8,128)(2,1)} %bitcast.15, ...), custom_call_target="tpu_custom_call" | custom-call | tf_op jit(solution)/shard_map/pallas_call | solution.py:1261

commit v5 on v4

--- a/solution.py
+++ b/solution.py
@@ -1036,8 +1036,9 @@
     both((grads, 0, oy), (grads, 1, y), (grads, 1, oy), (grads, 2, y), (g_y, 2), (grads, 2, oy), (grads, 3, y))
     both((g_y, 3), (grads, 3, oy))
     both((up_grads,))
+    both((bwd, 0, 4))
     end((pass1, 0))
-    both((bwd, 0, 8), (bwd_keys,))
+    both((bwd, 4, 8), (bwd_keys,))
     end((pass1, 1))
     both((qkv_grads,))
     both((wide_out, 0))

time: 123 us -> 123 us (level)
  no operation moved by 1% of the time
where the time goes in v5:
time: 123 us
  Pallas kernels  122 us (99%)
    pallas_call x1, Pallas kernels, fast_local(): pl.pallas_call(fused, out_shape=[shape((TOK, MODEL), BF16), shape((TOK, M...  118 us
    pallas_call x1, Pallas kernels, fast_local(): pl.pallas_call(finish, out_shape=[shape((TOK, MODEL), BF16), shape((TOK,...  3.65 us

profile of v5, /device:TPU:0, one launch (start us, length us, event | category | flops | bytes accessed | tf_op | source)
XLA Modules:
  0.0 122.7 jit_solution(5874530046374340653)
XLA Ops:
  0.6 118.2 %shard_map.212 = (bf16[128,1024]{1,0:T(8,128)(2,1)}, f32[128,1024]{1,0:T(8,128)}, f32[8,1024]{1,0:T(8,128)}, f32[160,1024]{1,0:T(8,128)}, bf16[2,16,32,256]{3,2,1,0:T(8,128)(2,1)}, /*index=5*/f32[8,128]{1,0:T(8,128)}) custom-call(bf16[128,1024]{1,0:T(8,128)(2,1)} %bitcast.14, bf16[128,1024]{1,0:T(8,128)(2,1)} %bitcast.16, bf16[32,3072]{1,0:T(8,128)(2,1)} %w_qkv_h.1, ...), custom_call_target="tpu_custom_call" | custom-call | tf_op jit(solution)/shard_map/pallas_call | solution.py:1181
  118.8 3.6 %shard_map.213 = (bf16[128,1024]{1,0:T(8,128)(2,1)}, f32[128,1024]{1,0:T(8,128)}, f32[1,32]{1,0:T(1,128)}, f32[1,32]{1,0:T(1,128)}, f32[32,3072]{1,0:T(8,128)}, ...) custom-call(bf16[128,1024]{1,0:T(8,128)(2,1)} %bitcast.15, ...), custom_call_target="tpu_custom_call" | custom-call | tf_op jit(solution)/shard_map/pallas_call | solution.py:1262

commit v6 on v5

--- a/solution.py
+++ b/solution.py
@@ -1049,9 +1049,7 @@
     both((norm_grads, 0, y), (norm_grads, 1, y), (norm_grads, 2, y), (norm_grads, 3, y))
     mid((pass1, 1), (pass1, 2))
     both((ln_grads,), (down_grads,))
-    both((wide_out, 1))
-    end((end1,), (pass2, 0), (ln_out,))
-    mid((ln_out,), (end1,), (pass2, 0))
+    both((wide_out, 1), (ln_out,), (end1,), (pass2, 0))
     both((pass2, 1))
     both((down_out,))
     both((pass2, 2), (ln_arrive,), (wide_arrive,), (end2,))

time: 123 us -> 123 us (level)
  no operation moved by 1% of the time
where the time goes in v6:
time: 123 us
  Pallas kernels  122 us (99%)
    pallas_call x1, Pallas kernels, fast_local(): pl.pallas_call(fused, out_shape=[shape((TOK, MODEL), BF16), shape((TOK, M...  118 us
    pallas_call x1, Pallas kernels, fast_local(): pl.pallas_call(finish, out_shape=[shape((TOK, MODEL), BF16), shape((TOK,...  3.65 us

profile of v6, /device:TPU:0, one launch (start us, length us, event | category | flops | bytes accessed | tf_op | source)
XLA Modules:
  0.0 122.8 jit_solution(4864586489981908038)
XLA Ops:
  0.6 118.4 %shard_map.212 = (bf16[128,1024]{1,0:T(8,128)(2,1)}, f32[128,1024]{1,0:T(8,128)}, f32[8,1024]{1,0:T(8,128)}, f32[160,1024]{1,0:T(8,128)}, bf16[2,16,32,256]{3,2,1,0:T(8,128)(2,1)}, /*index=5*/f32[8,128]{1,0:T(8,128)}) custom-call(bf16[128,1024]{1,0:T(8,128)(2,1)} %bitcast.14, bf16[128,1024]{1,0:T(8,128)(2,1)} %bitcast.16, bf16[32,3072]{1,0:T(8,128)(2,1)} %w_qkv_h.1, ...), custom_call_target="tpu_custom_call" | custom-call | tf_op jit(solution)/shard_map/pallas_call | solution.py:1179
  119.0 3.6 %shard_map.213 = (bf16[128,1024]{1,0:T(8,128)(2,1)}, f32[128,1024]{1,0:T(8,128)}, f32[1,32]{1,0:T(1,128)}, f32[1,32]{1,0:T(1,128)}, f32[32,3072]{1,0:T(8,128)}, ...) custom-call(bf16[128,1024]{1,0:T(8,128)(2,1)} %bitcast.15, ...), custom_call_target="tpu_custom_call" | custom-call | tf_op jit(solution)/shard_map/pallas_call | solution.py:1260
